TPU v7x, 32 devices: a whole 2x2x4 slice. The times are simulated.
32 devices in a mesh: prop: 16 (over z, y, x), trans: 2 (over core).
Axes of the slice: x: 2, y: 2, z: 4, core: 2. Of those that a mesh axis runs over, the one named last changes fastest.
Arguments:
- velocity: float32 [3, 128, 32, 128], P(None, 'prop', 'trans'), may hold values from -4 to 4
- stress: float32 [6, 128, 32, 128], P(None, 'prop', 'trans'), may hold values from -4 to 4
- density: float32 [12, 128, 32, 128], P(None, 'prop', 'trans'), may hold values from 0.5 to 2
- shear: float32 [128, 32, 128], P('prop', 'trans'), may hold values from 0.5 to 2
- normals: int32 [12, 3], replicated, may hold values from -2 to 2, as said below
- directions: int32 [12, 3], replicated, may hold values from -2 to 2, as said below
- inflow: float32 [21, 4, 32, 128], P(None, None, 'trans'), may hold values from -1.4 to 1.4
Outputs:
- velocity_out: float32 [3, 128, 32, 128], P(None, 'prop', 'trans')
- stress_out: float32 [6, 128, 32, 128], P(None, 'prop', 'trans')
- density_out: float32 [12, 128, 32, 128], P(None, 'prop', 'trans')
Inputs may be any that keep to these rules, and one draw needn't show every extreme that they name: `normals`: every entry of each normal is nonzero. `directions`: each direction has exactly one zero entry and is perpendicular to the normal of the same row.
All inputs are finite; a program needn't handle non-finite values.
Results may differ from a plain program's by a relative error of at most 0.00015.
Values sent between devices are 32-bit elements; how exact they have to be, the bound alone decides.
No kernel may reach another device: no remote copies, remote signals or barrier semaphores. Data moves between devices by JAX's collectives and lax.ppermute only.
A program may use at most 64 MiB of HBM per device.

v0:
```python
import functools

import jax
import jax.numpy as jnp
from jax import lax
from jax.experimental import pallas as pl
from jax.experimental.pallas import tpu as pltpu
from jax.sharding import PartitionSpec as P

STEPS = 4
ADV = 4
TIME_STEP = 0.15
DRAG_RATE = 0.5
HARDENING = 2.0
RECOVERY = 1.0
VOIGT_PAIRS = ((0, 0), (1, 1), (2, 2), (1, 2), (0, 2), (0, 1))
ACCEL = ((0, 5, 4), (5, 1, 3), (4, 3, 2))

PLANES = 8
ROWS = 16
TAIL = 8
EXT = ROWS + TAIL
LANES = 128
C1 = TIME_STEP / 12.0
C8 = 8.0 * TIME_STEP / 12.0
F32 = jnp.float32


def lane_shifts(x):
    lane = lax.broadcasted_iota(jnp.int32, x.shape, 1)

    def at(offset):
        moved = pltpu.roll(x, (-offset) % LANES, 1)
        inside = lane < LANES - offset if offset > 0 else lane >= -offset
        return jnp.where(inside, moved, 0.0)

    return at(1) - at(-1), at(2) - at(-2)


def row_shifts(x):
    size = x.shape[0]
    return (
        pltpu.roll(x, size - 1, 0) - pltpu.roll(x, 1, 0),
        pltpu.roll(x, size - 2, 0) - pltpu.roll(x, 2, 0),
    )


def extended(inner, tail):
    return jnp.concatenate([inner, tail], axis=0)


def edge_tile(plane):
    row = lax.broadcasted_iota(jnp.int32, (TAIL, LANES), 0)
    return jnp.where(row < 4, plane[:TAIL], plane[ROWS - TAIL :])


def plastic_parts(stress, densities, shear, tab_ref):
    doubled = [s if k < 3 else s + s for k, s in enumerate(stress)]
    total = [None] * 6
    grown = []
    for s in range(12):
        coef = [tab_ref[s, k] for k in range(6)]
        coef = [jnp.concatenate([c] * (stress[0].shape[0] // 8), axis=0) for c in coef]
        resolved = doubled[0] * coef[0]
        for k in range(1, 6):
            resolved = resolved + doubled[k] * coef[k]
        density = densities(s)
        rate = (DRAG_RATE * density) * jnp.tanh(resolved)
        for k in range(6):
            term = rate * coef[k]
            total[k] = term if total[k] is None else total[k] + term
        growth = (TIME_STEP * jnp.abs(rate)) * (HARDENING * lax.rsqrt(density) - RECOVERY)
        grown.append(density * jnp.exp(growth))
    scaled = TIME_STEP * shear
    dilation = scaled * (total[0] + total[1] + total[2])
    twice = 2.0 * scaled
    left = [stress[k] - twice * total[k] - (dilation if k < 3 else 0.0) for k in range(6)]
    return left, grown


def stress_change(near, velocity, shear):
    grad = [[None] * 3 for _ in range(3)]
    for c in range(3):
        first = near(c, 1) - near(c, -1)
        second = near(c, 2) - near(c, -2)
        grad[0][c] = 8.0 * first - second
        first, second = row_shifts(velocity[c])
        grad[1][c] = 8.0 * first[:ROWS] - second[:ROWS]
        first, second = lane_shifts(velocity[c][:ROWS])
        grad[2][c] = 8.0 * first - second
    scaled = C1 * shear
    trace = grad[0][0] + grad[1][1] + grad[2][2]
    return [
        scaled * (trace + 2.0 * grad[0][0]),
        scaled * (trace + 2.0 * grad[1][1]),
        scaled * (trace + 2.0 * grad[2][2]),
        scaled * (grad[1][2] + grad[2][1]),
        scaled * (grad[0][2] + grad[2][0]),
        scaled * (grad[0][1] + grad[1][0]),
    ]


def edges_kernel(v_ref, s_ref, edge_ref):
    for p in range(PLANES):
        for c in range(3):
            edge_ref[c, p] = edge_tile(v_ref[c, p])
        for k in range(6):
            edge_ref[3 + k, p] = edge_tile(s_ref[k, p])


def partial_update(p, v_ref, s_ref, rec_ref, below):
    out = []
    for c, (ix, iy, iz) in enumerate(ACCEL):

        def plane(k, q):
            return extended(s_ref[k, q], rec_ref[3 + k, q])

        along = extended(s_ref[iy, p], rec_ref[3 + iy, p] * below)
        first, second = row_shifts(along)
        f, s = lane_shifts(plane(iz, p))
        first, second = first + f, second + s
        if p + 1 < PLANES:
            first = first + plane(ix, p + 1)
        if p - 1 >= 0:
            first = first - plane(ix, p - 1)
        if p + 2 < PLANES:
            second = second + plane(ix, p + 2)
        if p - 2 >= 0:
            second = second - plane(ix, p - 2)
        start = extended(v_ref[c, p], rec_ref[c, p])
        out.append(start + C8 * first - C1 * second)
    return out


def first_kernel(v_ref, s_ref, rec_ref, mask_ref, w_ref, near_ref, far_ref):
    below = mask_ref[0]
    even = mask_ref[3] > 0.5
    for p in range(PLANES):
        made = partial_update(p, v_ref, s_ref, rec_ref, below)
        for c in range(3):
            w_ref[c, p] = made[c]
    for q in range(2):
        low, high = q, PLANES - 2 + q
        for c in range(3):
            for h in range(2):
                rows = pl.ds(8 * h, 8)
                left, right = w_ref[c, low, rows], w_ref[c, high, rows]
                near_ref[q, 2 * c + h] = jnp.where(even, right, left)
                far_ref[q, 2 * c + h] = jnp.where(even, left, right)
                left, right = s_ref[ACCEL[c][0], low, rows], s_ref[ACCEL[c][0], high, rows]
                near_ref[q, 6 + 3 * c + h] = jnp.where(even, right, left)
                far_ref[q, 6 + 3 * c + h] = jnp.where(even, left, right)
            left, right = rec_ref[3 + ACCEL[c][0], low], rec_ref[3 + ACCEL[c][0], high]
            near_ref[q, 6 + 3 * c + 2] = jnp.where(even, right, left)
            far_ref[q, 6 + 3 * c + 2] = jnp.where(even, left, right)


def plastic_kernel(ahead, s_ref, d_ref, shear_ref, tab_ref, left_ref, grown_ref, *send_ref):
    for p in range(PLANES):
        left, grown = plastic_parts(
            [s_ref[k, p] for k in range(6)], lambda s: d_ref[s, p], shear_ref[p], tab_ref
        )
        for k in range(6):
            left_ref[k, p] = left[k]
        for s in range(12):
            grown_ref[s, p] = grown[s]
            if ahead and p < ADV:
                send_ref[0][s, p] = grown[s]
        if ahead and p < ADV:
            send_ref[0][12, p] = shear_ref[p]


def second_kernel(
    w_ref, near_ref, far_ref, s_ref, left_ref, shear_ref, mask_ref, v_ref, out_ref, edge_ref, vel
):
    below, has_left, has_right = mask_ref[0], mask_ref[1], mask_ref[2]
    even = mask_ref[3] > 0.5

    def got(side, q, tile):
        a, b = near_ref[q, tile], far_ref[q, tile]
        return jnp.where(even, b, a) if side == 0 else jnp.where(even, a, b)

    def got_w(side, q, c):
        return jnp.concatenate([got(side, q, 2 * c + h) for h in range(2)], axis=0)

    def got_s(side, q, c):
        return jnp.concatenate([got(side, q, 6 + 3 * c + h) for h in range(3)], axis=0)

    exists = [jnp.concatenate([m, m], axis=0) for m in (has_left, has_right)]
    for c in range(3):
        ix = ACCEL[c][0]
        m2, m1, p8, p9 = got_s(0, 0, c), got_s(0, 1, c), got_s(1, 0, c), got_s(1, 1, c)
        for p in range(PLANES):
            value = w_ref[c, p]
            if p == 0:
                value = value - C8 * m1 + C1 * m2
            if p == 1:
                value = value + C1 * m1
            if p == 6:
                value = value - C1 * p8
            if p == 7:
                value = value + C8 * p8 - C1 * p9
            value = extended(value[:ROWS], value[ROWS:] * below)
            vel[c, p + 2] = value
            v_ref[c, p] = value[:ROWS]
            edge_ref[c, p] = edge_tile(value[:ROWS])
        none = jnp.zeros((TAIL, LANES), F32)
        halo = (
            (0, got_w(0, 0, c) - C1 * s_ref[ix, 0], 0),
            (1, got_w(0, 1, c) + C8 * s_ref[ix, 0] - C1 * s_ref[ix, 1], 0),
            (10, got_w(1, 0, c) - C8 * s_ref[ix, 7] + C1 * s_ref[ix, 6], 1),
            (11, got_w(1, 1, c) + C1 * s_ref[ix, 7], 1),
        )
        for at, value, side in halo:
            vel[c, at] = extended(value * exists[side], none)
    for p in range(PLANES):
        change = stress_change(
            lambda c, o: vel[c, p + 2 + o, pl.ds(0, ROWS)], [vel[c, p + 2] for c in range(3)], shear_ref[p]
        )
        for k in range(6):
            value = left_ref[k, p] + change[k]
            out_ref[k, p] = value
            edge_ref[3 + k, p] = edge_tile(value)


LAST_W, LAST_S, LAST_X, LAST_TILES = 0, 48, 96, 102


def last_first_kernel(v_ref, s_ref, rec_ref, mask_ref, w_ref, msg_ref):
    below = mask_ref[0]
    for p in range(PLANES):
        made = partial_update(p, v_ref, s_ref, rec_ref, below)
        for c in range(3):
            w_ref[c, p] = made[c]
            if p < 6:
                base = LAST_W + 16 * c + (3 * p if p < 4 else 12 + 2 * (p - 4))
                for h in range(3 if p < 4 else 2):
                    msg_ref[base + h] = made[c][8 * h : 8 * h + 8]
            if p < 2:
                msg_ref[LAST_X + 2 * c + p] = rec_ref[3 + ACCEL[c][0], p]
        if p < ADV:
            for k in range(6):
                for h in range(2):
                    msg_ref[LAST_S + 8 * k + 2 * p + h] = s_ref[k, p, pl.ds(8 * h, 8)]


def last_plastic_kernel(s_ref, d_ref, shear_ref, tab_ref, left_ref, grown_ref):
    for p in range(ADV, PLANES):
        left, grown = plastic_parts(
            [s_ref[k, p] for k in range(6)], lambda s: d_ref[s, p], shear_ref[p], tab_ref
        )
        for k in range(6):
            left_ref[k, p - ADV] = left[k]
        for s in range(12):
            grown_ref[s, p - ADV] = grown[s]


def last_second_kernel(
    w_ref, msg_ref, more_ref, s_ref, rec_ref, left_ref, grown_ref, shear_ref, tab_ref, mask_ref, inflow_ref,
    v_ref, out_ref, d_ref, vel,
):
    below = mask_ref[0]
    here = jnp.concatenate([mask_ref[2]] * 2, axis=0)
    inside = here > 0.5

    def got(base, count):
        return jnp.concatenate([msg_ref[base + h] for h in range(count)], axis=0)

    def got_stress(k, p):
        return got(LAST_S + 8 * k + 2 * p, 2)

    for c in range(3):
        ix = ACCEL[c][0]
        p8 = extended(got_stress(ix, 0), msg_ref[LAST_X + 2 * c])
        p9 = extended(got_stress(ix, 1), msg_ref[LAST_X + 2 * c + 1])
        p6 = extended(s_ref[ix, 6], rec_ref[3 + ix, 6])
        p7 = extended(s_ref[ix, 7], rec_ref[3 + ix, 7])
        for p in range(2, 14):
            if p < PLANES:
                value = w_ref[c, p]
                if p == 6:
                    value = value - C1 * p8
                if p == 7:
                    value = value + C8 * p8 - C1 * p9
            elif p < 12:
                value = got(LAST_W + 16 * c + 3 * (p - 8), 3)
                if p == 8:
                    value = value - C8 * p7 + C1 * p6
                if p == 9:
                    value = value + C1 * p7
            else:
                value = got(LAST_W + 16 * c + 12 + 2 * (p - 12), 2)
            inner = value[:ROWS]
            tail = value[ROWS:] * below if p < 12 else jnp.zeros((TAIL, LANES), F32)
            if p >= PLANES:
                inner, tail = inner * here, tail * mask_ref[2]
            vel[c, p - 2] = extended(inner, tail)
            if ADV <= p < 12:
                if p >= PLANES:
                    inner = jnp.where(inside, inner, inflow_ref[c, p - PLANES])
                v_ref[c, p - ADV] = inner
    for q in range(PLANES):
        p = q + ADV
        if p < PLANES:
            left = [left_ref[k, q] for k in range(6)]
            grown = [grown_ref[s, q] for s in range(12)]
            shear = shear_ref[p]
        else:
            r = p - PLANES
            shear = more_ref[12, r]
            left, grown = plastic_parts(
                [got_stress(k, r) for k in range(6)], lambda s: more_ref[s, r], shear, tab_ref
            )
        change = stress_change(
            lambda c, o: vel[c, p - 2 + o, pl.ds(0, ROWS)], [vel[c, p - 2] for c in range(3)], shear
        )
        for k in range(6):
            value = left[k] + change[k]
            if p >= PLANES:
                value = jnp.where(inside, value, inflow_ref[3 + k, p - PLANES])
            out_ref[k, q] = value
        for s in range(12):
            value = grown[s]
            if p >= PLANES:
                value = jnp.where(inside, value, inflow_ref[9 + s, p - PLANES])
            d_ref[s, q] = value


VMEM_LIMIT = 16 * 2**20


def call(kernel, outs, args, scratch=(), flops=0):
    return pl.pallas_call(
        kernel,
        out_shape=[jax.ShapeDtypeStruct(shape, F32) for shape in outs],
        scratch_shapes=[pltpu.VMEM(shape, F32) for shape in scratch],
        compiler_params=pltpu.CompilerParams(vmem_limit_bytes=VMEM_LIMIT),
        cost_estimate=pl.CostEstimate(flops=flops, bytes_accessed=2**20, transcendentals=0),
    )(*args)


def schmid_table(normals, directions):
    normal_f = normals.astype(F32)
    direct_f = directions.astype(F32)
    scale = 1.0 / (
        jnp.sqrt(jnp.sum(normal_f * normal_f, 1)) * jnp.sqrt(jnp.sum(direct_f * direct_f, 1))
    )
    columns = [
        0.5 * (direct_f[:, i] * normal_f[:, j] + direct_f[:, j] * normal_f[:, i]) * scale
        for i, j in VOIGT_PAIRS
    ]
    return jnp.stack(columns, 1)


def swap_rows(edge):
    count = lax.axis_size("trans")
    if count == 2:
        return lax.ppermute(edge, "trans", [(0, 1), (1, 0)])
    upper = lax.ppermute(edge[:, :, :4], "trans", [(i + 1, i) for i in range(count - 1)])
    lower = lax.ppermute(edge[:, :, 4:], "trans", [(i, i + 1) for i in range(count - 1)])
    return jnp.concatenate([upper, lower], axis=2)


def local(velocity, stress, density, shear, normals, directions, inflow):
    count = lax.axis_size("prop")
    at, side = lax.axis_index("prop"), lax.axis_index("trans")
    table = jnp.broadcast_to(schmid_table(normals, directions)[:, :, None, None], (12, 6, 8, LANES))
    row = lax.broadcasted_iota(jnp.int32, (TAIL, LANES), 0)
    full = jnp.ones((TAIL, LANES), F32)
    masks = jnp.stack(
        [
            jnp.where(row < 4, side < lax.axis_size("trans") - 1, side > 0).astype(F32),
            full * (at > 0).astype(F32),
            full * (at < count - 1).astype(F32),
            full * (at % 2 == 0).astype(F32),
        ]
    )
    pairs = [(i, i + 1) for i in range(0, count - 1, 2)]
    others = [(i, i + 1) for i in range(1, count - 1, 2)]
    pairs, others = ([(a, b) for a, b in p] + [(b, a) for a, b in p] for p in (pairs, others))

    shape = (PLANES, ROWS, LANES)
    wide = (3, PLANES, EXT, LANES)
    edge_shape = (9, PLANES, TAIL, LANES)
    (edge,) = call(edges_kernel, [edge_shape], (velocity, stress))
    for step in range(STEPS - 1):
        rec = swap_rows(edge)
        message = (2, 15, 8, LANES)
        w, near, far = call(first_kernel, [wide, message, message], (velocity, stress, rec, masks))
        far = lax.ppermute(far, "prop", others)
        near = lax.ppermute(near, "prop", pairs)
        ahead = step == STEPS - 2
        made = call(
            functools.partial(plastic_kernel, ahead),
            [(6, *shape), (12, *shape)] + ([(13, ADV, ROWS, LANES)] if ahead else []),
            (stress, density, shear, table),
            flops=2**24,
        )
        left, density = made[:2]
        if ahead:
            more = lax.ppermute(made[2], "prop", [(i + 1, i) for i in range(count - 1)])
        velocity, stress, edge = call(
            second_kernel,
            [(3, *shape), (6, *shape), edge_shape],
            (w, near, far, stress, left, shear, masks),
            scratch=[(3, PLANES + 4, EXT, LANES)],
        )
    rec = swap_rows(edge)
    w, message = call(
        last_first_kernel, [wide, (LAST_TILES, 8, LANES)], (velocity, stress, rec, masks)
    )
    message = lax.ppermute(message, "prop", [(i + 1, i) for i in range(count - 1)])
    half = (ADV, ROWS, LANES)
    left, grown = call(
        last_plastic_kernel, [(6, *half), (12, *half)], (stress, density, shear, table), flops=2**23
    )
    return tuple(
        call(
            last_second_kernel,
            [(3, *shape), (6, *shape), (12, *shape)],
            (w, message, more, stress, rec, left, grown, shear, table, masks, inflow),
            scratch=[(3, PLANES + 4, EXT, LANES)],
        )
    )


def solution(mesh):
    return jax.shard_map(
        local,
        mesh=mesh,
        in_specs=(
            P(None, "prop", "trans", None),
            P(None, "prop", "trans", None),
            P(None, "prop", "trans", None),
            P("prop", "trans", None),
            P(),
            P(),
            P(None, None, "trans", None),
        ),
        out_specs=(
            P(None, "prop", "trans", None),
            P(None, "prop", "trans", None),
            P(None, "prop", "trans", None),
        ),
        check_vma=False,
    )
```

profile of v0, /device:TPU:14, one launch (start us, length us, event | category | flops | bytes accessed | tf_op | source)
XLA Modules:
  0.0 64.6 jit_solution(2352939674065867572)
XLA Ops:
  0.6 1.0 %copy-done = f32[6,8,16,128]{3,2,1,0:T(8,128)S(1)} copy-done((f32[6,8,16,128]{3,2,1,0:T(8,128)S(1)}, f32[6,8,16,128]{3,2,1,0:T(8,128)}, u32[]{:S(2)}) %copy-start) | copy-done | bytes 393240
  1.6 0.9 %copy-done.3 = f32[3,8,16,128]{3,2,1,0:T(8,128)S(1)} copy-done((f32[3,8,16,128]{3,2,1,0:T(8,128)S(1)}, f32[3,8,16,128]{3,2,1,0:T(8,128)}, u32[]{:S(2)}) %copy-start.3) | copy-done | bytes 196632
  2.7 0.5 copy-done.7
  3.7 0.6 collective-permute-done.rec_ref
  4.7 0.6 collective-permute-start.1
  5.3 4.3 %collective-permute-start.2 = (f32[2,15,8,128]{3,2,1,0:T(8,128)S(1)}, f32[2,15,8,128]{3,2,1,0:T(8,128)S(1)}, u32[]{:S(2)}, u32[]{:S(2)}) collective-permute-start(f32[2,15,8,128]{3,2,1,0:T(8,128)S(1)} %get-tuple-element.34), channel_id=1, source_target_pairs={{2,4},{6,8},{10,12},{14,16},{18,20},{22,24},{26,28},{4,2},{8,6},{1... | collective-permute-start | bytes 368648 | tf_op jit(solution)/shard_map/ppermute | solution.py:390
  9.9 0.7 %copy-done.2 = f32[8,16,128]{2,1,0:T(8,128)S(1)} copy-done((f32[8,16,128]{2,1,0:T(8,128)S(1)}, f32[8,16,128]{2,1,0:T(8,128)}, u32[]{:S(2)}) %copy-start.2) | copy-done | bytes 65560
  10.6 1.0 %shard_map.96 = (f32[6,8,16,128]{3,2,1,0:T(8,128)S(1)}, f32[12,8,16,128]{3,2,1,0:T(8,128)S(1)}) custom-call(f32[6,8,16,128]{3,2,1,0:T(8,128)S(1)} %copy-done.1, f32[12,8,16,128]{3,2,1,0:T(8,128)S(1)} %copy-done.5, f32[8,16,128]{2,1,0:T(8,128)S(1)} %copy-done.2, f32[12,6,8,128]{3,2,1,0:T(8,128)S(1)} %broadcast_in_dim.16.tab_ref), custom_call_target="tpu_custom_call" | custom-call | flops 16777216 | bytes 1048576 | tf_op jit(solution)/shard_map/pallas_call | solution.py:333
  11.6 2.4 %collective-permute-done.2.far_ref = f32[2,15,8,128]{3,2,1,0:T(8,128)S(1)} collective-permute-done((f32[2,15,8,128]{3,2,1,0:T(8,128)S(1)}, f32[2,15,8,128]{3,2,1,0:T(8,128)S(1)}, u32[]{:S(2)}, u32[]{:S(2)}) %collective-permute-start.2) | collective-permute-done | bytes 122912 | tf_op jit(solution)/shard_map/ppermute | solution.py:390
  14.4 1.6 %collective-permute-done.3.rec_ref = f32[9,8,8,128]{3,2,1,0:T(8,128)S(1)} collective-permute-done((f32[9,8,8,128]{3,2,1,0:T(8,128)S(1)}, f32[9,8,8,128]{3,2,1,0:T(8,128)S(1)}, u32[]{:S(2)}, u32[]{:S(2)}) %collective-permute-start.3) | collective-permute-done | bytes 294944 | tf_op jit(solution)/shard_map/ppermute | solution.py:358
  16.3 0.7 %collective-permute-start.4 = (f32[2,15,8,128]{3,2,1,0:T(8,128)S(1)}, f32[2,15,8,128]{3,2,1,0:T(8,128)S(1)}, u32[]{:S(2)}, u32[]{:S(2)}) collective-permute-start(f32[2,15,8,128]{3,2,1,0:T(8,128)S(1)} %get-tuple-element.40), channel_id=1, source_target_pairs={{0,2},{4,6},{8,10},{12,14},{16,18},{20,22},{24,26},{28,30},{2,0},{... | collective-permute-start | bytes 368648 | tf_op jit(solution)/shard_map/ppermute | solution.py:391
  17.0 3.9 %collective-permute-start.5 = (f32[2,15,8,128]{3,2,1,0:T(8,128)S(1)}, f32[2,15,8,128]{3,2,1,0:T(8,128)S(1)}, u32[]{:S(2)}, u32[]{:S(2)}) collective-permute-start(f32[2,15,8,128]{3,2,1,0:T(8,128)S(1)} %get-tuple-element.41), channel_id=1, source_target_pairs={{2,4},{6,8},{10,12},{14,16},{18,20},{22,24},{26,28},{4,2},{8,6},{1... | collective-permute-start | bytes 368648 | tf_op jit(solution)/shard_map/ppermute | solution.py:390
  21.0 1.0 %shard_map.99 = (f32[6,8,16,128]{3,2,1,0:T(8,128)S(1)}, f32[12,8,16,128]{3,2,1,0:T(8,128)S(1)}) custom-call(f32[6,8,16,128]{3,2,1,0:T(8,128)S(1)} %get-tuple-element.37.s_ref, f32[12,8,16,128]{3,2,1,0:T(8,128)S(1)} %get-tuple-element.42.d_ref, f32[8,16,128]{2,1,0:T(8,128)S(1)} %copy-done.2, f32[12,6,8,128]{3,2,1,0:T(8,128)S(1)} %broadcast_in_dim.16.tab_ref), custom_call_target="tpu_custom_call" | custom-call | flops 16777216 | bytes 1048576 | tf_op jit(solution)/shard_map/pallas_call | solution.py:333
  22.0 3.8 %collective-permute-done.5.far_ref = f32[2,15,8,128]{3,2,1,0:T(8,128)S(1)} collective-permute-done((f32[2,15,8,128]{3,2,1,0:T(8,128)S(1)}, f32[2,15,8,128]{3,2,1,0:T(8,128)S(1)}, u32[]{:S(2)}, u32[]{:S(2)}) %collective-permute-start.5) | collective-permute-done | bytes 122912 | tf_op jit(solution)/shard_map/ppermute | solution.py:390
  26.1 1.6 %collective-permute-done.6.rec_ref = f32[9,8,8,128]{3,2,1,0:T(8,128)S(1)} collective-permute-done((f32[9,8,8,128]{3,2,1,0:T(8,128)S(1)}, f32[9,8,8,128]{3,2,1,0:T(8,128)S(1)}, u32[]{:S(2)}, u32[]{:S(2)}) %collective-permute-start.6) | collective-permute-done | bytes 294944 | tf_op jit(solution)/shard_map/ppermute | solution.py:358
  28.1 0.6 collective-permute-start.7
  28.7 4.3 %collective-permute-start.8 = (f32[2,15,8,128]{3,2,1,0:T(8,128)S(1)}, f32[2,15,8,128]{3,2,1,0:T(8,128)S(1)}, u32[]{:S(2)}, u32[]{:S(2)}) collective-permute-start(f32[2,15,8,128]{3,2,1,0:T(8,128)S(1)} %get-tuple-element.49), channel_id=1, source_target_pairs={{2,4},{6,8},{10,12},{14,16},{18,20},{22,24},{26,28},{4,2},{8,6},{1... | collective-permute-start | bytes 368648 | tf_op jit(solution)/shard_map/ppermute | solution.py:390
  33.1 1.0 %shard_map.102 = (f32[6,8,16,128]{3,2,1,0:T(8,128)S(1)}, f32[12,8,16,128]{3,2,1,0:T(8,128)S(1)}, f32[13,4,16,128]{3,2,1,0:T(8,128)S(1)}) custom-call(f32[6,8,16,128]{3,2,1,0:T(8,128)S(1)} %get-tuple-element.45.s_ref, f32[12,8,16,128]{3,2,1,0:T(8,128)S(1)} %get-tuple-element.50.d_ref, f32[8,16,128]{2,1,0:T(8,128)S(1)} %copy-done.2, ...), custom_call_target="tpu_custom_call" | custom-call | flops 16777216 | bytes 1048576 | tf_op jit(solution)/shard_map/pallas_call | solution.py:333
  34.1 3.4 %collective-permute-done.8.far_ref = f32[2,15,8,128]{3,2,1,0:T(8,128)S(1)} collective-permute-done((f32[2,15,8,128]{3,2,1,0:T(8,128)S(1)}, f32[2,15,8,128]{3,2,1,0:T(8,128)S(1)}, u32[]{:S(2)}, u32[]{:S(2)}) %collective-permute-start.8) | collective-permute-done | bytes 122912 | tf_op jit(solution)/shard_map/ppermute | solution.py:390
  37.9 2.5 %collective-permute-start.11 = (f32[13,4,16,128]{3,2,1,0:T(8,128)S(1)}, f32[13,4,16,128]{3,2,1,0:T(8,128)S(1)}, u32[]{:S(2)}, u32[]{:S(2)}) collective-permute-start(f32[13,4,16,128]{3,2,1,0:T(8,128)S(1)} %get-tuple-element.57), channel_id=1, source_target_pairs={{2,0},{4,2},{6,4},{8,6},{10,8},{12,10},{14,12},{16,14},{18,16},{20... | collective-permute-start | bytes 1277960 | tf_op jit(solution)/shard_map/ppermute | solution.py:401
  40.8 3.1 %collective-permute-start.10 = (f32[102,8,128]{2,1,0:T(8,128)S(1)}, f32[102,8,128]{2,1,0:T(8,128)S(1)}, u32[]{:S(2)}, u32[]{:S(2)}) collective-permute-start(f32[102,8,128]{2,1,0:T(8,128)S(1)} %get-tuple-element.56), channel_id=1, source_target_pairs={{2,0},{4,2},{6,4},{8,6},{10,8},{12,10},{14,12},{16,14},{18,16},{20... | collective-permute-start | bytes 1253384 | tf_op jit(solution)/shard_map/ppermute | solution.py:412
  44.3 9.8 %collective-permute-done.11.more_ref = f32[13,4,16,128]{3,2,1,0:T(8,128)S(1)} collective-permute-done((f32[13,4,16,128]{3,2,1,0:T(8,128)S(1)}, f32[13,4,16,128]{3,2,1,0:T(8,128)S(1)}, u32[]{:S(2)}, u32[]{:S(2)}) %collective-permute-start.11) | collective-permute-done | bytes 426016 | tf_op jit(solution)/shard_map/ppermute | solution.py:401
  54.2 8.5 %collective-permute-done.10.msg_ref = f32[102,8,128]{2,1,0:T(8,128)S(1)} collective-permute-done((f32[102,8,128]{2,1,0:T(8,128)S(1)}, f32[102,8,128]{2,1,0:T(8,128)S(1)}, u32[]{:S(2)}, u32[]{:S(2)}) %collective-permute-start.10) | collective-permute-done | bytes 417824 | tf_op jit(solution)/shard_map/ppermute | solution.py:412
  62.7 1.8 %shard_map.106 = (f32[3,8,16,128]{3,2,1,0:T(8,128)}, f32[6,8,16,128]{3,2,1,0:T(8,128)}, f32[12,8,16,128]{3,2,1,0:T(8,128)}) custom-call(f32[3,8,24,128]{3,2,1,0:T(8,128)S(1)} %get-tuple-element.55.w_ref, f32[102,8,128]{2,1,0:T(8,128)S(1)} %collective-permute-done.10.msg_ref, f32[13,4,16,128]{3,2,1,0:T(8,128)S(1)} %collective-permute-done.11.more_ref, ...), custom_call_target="tpu_custom_call" | custom-call | bytes 1048576 | tf_op jit(solution)/shard_map/pallas_call | solution.py:333
  (45 shorter events, 4.0 us)
Async XLA Ops:
  0.6 1.0 %copy-start = (f32[6,8,16,128]{3,2,1,0:T(8,128)S(1)}, f32[6,8,16,128]{3,2,1,0:T(8,128)}, u32[]{:S(2)}) copy-start(f32[6,8,16,128]{3,2,1,0:T(8,128)} %s_ref.7) | copy-start | bytes 1179652
  1.6 0.9 %copy-start.3 = (f32[3,8,16,128]{3,2,1,0:T(8,128)S(1)}, f32[3,8,16,128]{3,2,1,0:T(8,128)}, u32[]{:S(2)}) copy-start(f32[3,8,16,128]{3,2,1,0:T(8,128)} %v_ref.3) | copy-start | bytes 589828
  2.6 0.7 %copy-start.7 = (s32[12,3]{0,1:T(4,128)S(1)}, s32[12,3]{0,1:T(4,128)}, u32[]{:S(2)}) copy-start(s32[12,3]{0,1:T(4,128)} %param.11) | copy-start | bytes 436
  2.6 0.7 %copy-start.8 = (s32[12,3]{0,1:T(4,128)S(1)}, s32[12,3]{0,1:T(4,128)}, u32[]{:S(2)}) copy-start(s32[12,3]{0,1:T(4,128)} %param.12) | copy-start | bytes 436
  2.6 1.7 %copy-start.1 = (f32[6,8,16,128]{3,2,1,0:T(8,128)S(1)}, f32[6,8,16,128]{3,2,1,0:T(8,128)}, u32[]{:S(2)}) copy-start(f32[6,8,16,128]{3,2,1,0:T(8,128)} %s_ref.7) | copy-start | bytes 1179652
  2.6 1.7 %copy-start.4 = (f32[3,8,16,128]{3,2,1,0:T(8,128)S(1)}, f32[3,8,16,128]{3,2,1,0:T(8,128)}, u32[]{:S(2)}) copy-start(f32[3,8,16,128]{3,2,1,0:T(8,128)} %v_ref.3) | copy-start | bytes 589828
  2.6 7.3 %copy-start.5 = (f32[12,8,16,128]{3,2,1,0:T(8,128)S(1)}, f32[12,8,16,128]{3,2,1,0:T(8,128)}, u32[]{:S(2)}) copy-start(f32[12,8,16,128]{3,2,1,0:T(8,128)} %d_ref.1) | copy-start | bytes 2359300
  2.6 1.6 %collective-permute-start = (f32[9,8,8,128]{3,2,1,0:T(8,128)S(1)}, f32[9,8,8,128]{3,2,1,0:T(8,128)S(1)}, u32[]{:S(2)}, u32[]{:S(2)}) collective-permute-start(f32[9,8,8,128]{3,2,1,0:T(8,128)S(1)} %shard_map.94), channel_id=1, source_target_pairs={{0,1},{1,0},{2,3},{3,2},{4,5},{5,4},{6,7},{7,6},{8,9},{9,8},{10,11... | collective-permute-start | bytes 884744 | tf_op jit(solution)/shard_map/ppermute | solution.py:358
  4.7 6.9 %collective-permute-start.1 = (f32[2,15,8,128]{3,2,1,0:T(8,128)S(1)}, f32[2,15,8,128]{3,2,1,0:T(8,128)S(1)}, u32[]{:S(2)}, u32[]{:S(2)}) collective-permute-start(f32[2,15,8,128]{3,2,1,0:T(8,128)S(1)} %get-tuple-element.33), channel_id=1, source_target_pairs={{0,2},{4,6},{8,10},{12,14},{16,18},{20,22},{24,26},{28,30},{2,0},{... | collective-permute-start | bytes 368648 | tf_op jit(solution)/shard_map/ppermute | solution.py:391
  5.3 8.8 %collective-permute-start.2 = (f32[2,15,8,128]{3,2,1,0:T(8,128)S(1)}, f32[2,15,8,128]{3,2,1,0:T(8,128)S(1)}, u32[]{:S(2)}, u32[]{:S(2)}) collective-permute-start(f32[2,15,8,128]{3,2,1,0:T(8,128)S(1)} %get-tuple-element.34), channel_id=1, source_target_pairs={{2,4},{6,8},{10,12},{14,16},{18,20},{22,24},{26,28},{4,2},{8,6},{1... | collective-permute-start | bytes 368648 | tf_op jit(solution)/shard_map/ppermute | solution.py:390
  9.7 0.8 %copy-start.2 = (f32[8,16,128]{2,1,0:T(8,128)S(1)}, f32[8,16,128]{2,1,0:T(8,128)}, u32[]{:S(2)}) copy-start(f32[8,16,128]{2,1,0:T(8,128)} %shear_ref.15) | copy-start | bytes 196612
  14.3 1.6 %collective-permute-start.3 = (f32[9,8,8,128]{3,2,1,0:T(8,128)S(1)}, f32[9,8,8,128]{3,2,1,0:T(8,128)S(1)}, u32[]{:S(2)}, u32[]{:S(2)}) collective-permute-start(f32[9,8,8,128]{3,2,1,0:T(8,128)S(1)} %get-tuple-element.38), channel_id=1, source_target_pairs={{0,1},{1,0},{2,3},{3,2},{4,5},{5,4},{6,7},{7,6},{8,9},{9,8},{10,11... | collective-permute-start | bytes 884744 | tf_op jit(solution)/shard_map/ppermute | solution.py:358
  16.3 5.6 %collective-permute-start.4 = (f32[2,15,8,128]{3,2,1,0:T(8,128)S(1)}, f32[2,15,8,128]{3,2,1,0:T(8,128)S(1)}, u32[]{:S(2)}, u32[]{:S(2)}) collective-permute-start(f32[2,15,8,128]{3,2,1,0:T(8,128)S(1)} %get-tuple-element.40), channel_id=1, source_target_pairs={{0,2},{4,6},{8,10},{12,14},{16,18},{20,22},{24,26},{28,30},{2,0},{... | collective-permute-start | bytes 368648 | tf_op jit(solution)/shard_map/ppermute | solution.py:391
  17.0 8.8 %collective-permute-start.5 = (f32[2,15,8,128]{3,2,1,0:T(8,128)S(1)}, f32[2,15,8,128]{3,2,1,0:T(8,128)S(1)}, u32[]{:S(2)}, u32[]{:S(2)}) collective-permute-start(f32[2,15,8,128]{3,2,1,0:T(8,128)S(1)} %get-tuple-element.41), channel_id=1, source_target_pairs={{2,4},{6,8},{10,12},{14,16},{18,20},{22,24},{26,28},{4,2},{8,6},{1... | collective-permute-start | bytes 368648 | tf_op jit(solution)/shard_map/ppermute | solution.py:390
  26.1 1.6 %collective-permute-start.6 = (f32[9,8,8,128]{3,2,1,0:T(8,128)S(1)}, f32[9,8,8,128]{3,2,1,0:T(8,128)S(1)}, u32[]{:S(2)}, u32[]{:S(2)}) collective-permute-start(f32[9,8,8,128]{3,2,1,0:T(8,128)S(1)} %get-tuple-element.46), channel_id=1, source_target_pairs={{0,1},{1,0},{2,3},{3,2},{4,5},{5,4},{6,7},{7,6},{8,9},{9,8},{10,11... | collective-permute-start | bytes 884744 | tf_op jit(solution)/shard_map/ppermute | solution.py:358
  28.1 5.9 %collective-permute-start.7 = (f32[2,15,8,128]{3,2,1,0:T(8,128)S(1)}, f32[2,15,8,128]{3,2,1,0:T(8,128)S(1)}, u32[]{:S(2)}, u32[]{:S(2)}) collective-permute-start(f32[2,15,8,128]{3,2,1,0:T(8,128)S(1)} %get-tuple-element.48), channel_id=1, source_target_pairs={{0,2},{4,6},{8,10},{12,14},{16,18},{20,22},{24,26},{28,30},{2,0},{... | collective-permute-start | bytes 368648 | tf_op jit(solution)/shard_map/ppermute | solution.py:391
  28.7 8.8 %collective-permute-start.8 = (f32[2,15,8,128]{3,2,1,0:T(8,128)S(1)}, f32[2,15,8,128]{3,2,1,0:T(8,128)S(1)}, u32[]{:S(2)}, u32[]{:S(2)}) collective-permute-start(f32[2,15,8,128]{3,2,1,0:T(8,128)S(1)} %get-tuple-element.49), channel_id=1, source_target_pairs={{2,4},{6,8},{10,12},{14,16},{18,20},{22,24},{26,28},{4,2},{8,6},{1... | collective-permute-start | bytes 368648 | tf_op jit(solution)/shard_map/ppermute | solution.py:390
  37.8 2.6 %collective-permute-start.9 = (f32[9,8,8,128]{3,2,1,0:T(8,128)S(1)}, f32[9,8,8,128]{3,2,1,0:T(8,128)S(1)}, u32[]{:S(2)}, u32[]{:S(2)}) collective-permute-start(f32[9,8,8,128]{3,2,1,0:T(8,128)S(1)} %get-tuple-element.54), channel_id=1, source_target_pairs={{0,1},{1,0},{2,3},{3,2},{4,5},{5,4},{6,7},{7,6},{8,9},{9,8},{10,11... | collective-permute-start | bytes 884744 | tf_op jit(solution)/shard_map/ppermute | solution.py:358
  37.9 16.3 %collective-permute-start.11 = (f32[13,4,16,128]{3,2,1,0:T(8,128)S(1)}, f32[13,4,16,128]{3,2,1,0:T(8,128)S(1)}, u32[]{:S(2)}, u32[]{:S(2)}) collective-permute-start(f32[13,4,16,128]{3,2,1,0:T(8,128)S(1)} %get-tuple-element.57), channel_id=1, source_target_pairs={{2,0},{4,2},{6,4},{8,6},{10,8},{12,10},{14,12},{16,14},{18,16},{20... | collective-permute-start | bytes 1277960 | tf_op jit(solution)/shard_map/ppermute | solution.py:401
  40.8 21.9 %collective-permute-start.10 = (f32[102,8,128]{2,1,0:T(8,128)S(1)}, f32[102,8,128]{2,1,0:T(8,128)S(1)}, u32[]{:S(2)}, u32[]{:S(2)}) collective-permute-start(f32[102,8,128]{2,1,0:T(8,128)S(1)} %get-tuple-element.56), channel_id=1, source_target_pairs={{2,0},{4,2},{6,4},{8,6},{10,8},{12,10},{14,12},{16,14},{18,16},{20... | collective-permute-start | bytes 1253384 | tf_op jit(solution)/shard_map/ppermute | solution.py:412
  43.8 18.9 %copy-start.6 = (f32[21,4,16,128]{3,2,1,0:T(8,128)S(1)}, f32[21,4,16,128]{3,2,1,0:T(8,128)}, u32[]{:S(2)}) copy-start(f32[21,4,16,128]{3,2,1,0:T(8,128)} %inflow_ref.1) | copy-start | bytes 2064388
where the time goes:
time: 64.9 us; the launch traced here: 64.6 us
  waiting for transfers between devices  31.7 us (49%)
  starting transfers between devices  20.3 us (31%)
  Pallas kernels  7.74 us (12%)
  local copies, waits for them, and re-layouts  3.71 us (6%)
  between operations  0.92 us (1%)
    ppermute x3, starting transfers between devices, local(): far = lax.ppermute(far, 'prop', others)  12.6 us
    ppermute x1, waiting for transfers between devices, local(): more = lax.ppermute(made[2], 'prop', [(i + 1, i) for i in range(count - 1)])  9.82 us
    ppermute x3, waiting for transfers between devices, local(): far = lax.ppermute(far, 'prop', others)  9.65 us
    ppermute x1, waiting for transfers between devices, local(): lax.ppermute(message, 'prop', [(i + 1, i) for i in range(count - 1)])  8.55 us
    pallas_call x13, Pallas kernels, call(): pl.pallas_call(kernel, out_shape=[jax.ShapeDtypeStruct(shape, F32) for sh...  7.74 us
    ppermute x4, waiting for transfers between devices, swap_rows(): return lax.ppermute(edge, 'trans', [(0, 1), (1, 0)])  3.7 us
    unnamed x18, local copies, waits for them, and re-layouts  3.17 us
    ppermute x1, starting transfers between devices, local(): lax.ppermute(message, 'prop', [(i + 1, i) for i in range(count - 1)])  3.06 us
  transfers between devices with their start and end apart: 12, of which 8 were waited for; matrix products, arithmetic and copies ran while one was open for 1% of the time, Pallas kernels for 6%

commit v1 on v0

--- a/solution.py
+++ b/solution.py
@@ -52,6 +52,15 @@
 def edge_tile(plane):
     row = lax.broadcasted_iota(jnp.int32, (TAIL, LANES), 0)
     return jnp.where(row < 4, plane[:TAIL], plane[ROWS - TAIL :])
+
+
+def two_tails(a, b):
+    row = lax.broadcasted_iota(jnp.int32, (TAIL, LANES), 0)
+    return jnp.where((row < 2) | (row >= 6), a, pltpu.roll(b, 4, 0))
+
+
+def second_tail(tile):
+    return pltpu.roll(tile, 4, 0)
 
 
 def plastic_parts(stress, densities, shear, tab_ref):
@@ -100,12 +109,15 @@
     ]
 
 
-def edges_kernel(v_ref, s_ref, edge_ref):
-    for p in range(PLANES):
-        for c in range(3):
-            edge_ref[c, p] = edge_tile(v_ref[c, p])
-        for k in range(6):
-            edge_ref[3 + k, p] = edge_tile(s_ref[k, p])
+def edges_kernel(v_in, s_in, edge_ref, v_ref, s_ref, sems):
+    copies = [pltpu.make_async_copy(v_in.at[c], v_ref.at[c], sems.at[c]) for c in range(3)]
+    copies += [pltpu.make_async_copy(s_in.at[k], s_ref.at[k], sems.at[3 + k]) for k in range(6)]
+    for copy in copies:
+        copy.start()
+    for k, copy in enumerate(copies):
+        copy.wait()
+        for p in range(PLANES):
+            edge_ref[k, p] = edge_tile(v_ref[k, p] if k < 3 else s_ref[k - 3, p])
 
 
 def partial_update(p, v_ref, s_ref, rec_ref, below):
@@ -139,20 +151,20 @@
         made = partial_update(p, v_ref, s_ref, rec_ref, below)
         for c in range(3):
             w_ref[c, p] = made[c]
-    for q in range(2):
-        low, high = q, PLANES - 2 + q
-        for c in range(3):
+    def both(tile, left, right):
+        near_ref[tile] = jnp.where(even, right, left)
+        far_ref[tile] = jnp.where(even, left, right)
+
+    low, high = (0, 1), (PLANES - 2, PLANES - 1)
+    for c in range(3):
+        k = ACCEL[c][0]
+        for q in range(2):
             for h in range(2):
                 rows = pl.ds(8 * h, 8)
-                left, right = w_ref[c, low, rows], w_ref[c, high, rows]
-                near_ref[q, 2 * c + h] = jnp.where(even, right, left)
-                far_ref[q, 2 * c + h] = jnp.where(even, left, right)
-                left, right = s_ref[ACCEL[c][0], low, rows], s_ref[ACCEL[c][0], high, rows]
-                near_ref[q, 6 + 3 * c + h] = jnp.where(even, right, left)
-                far_ref[q, 6 + 3 * c + h] = jnp.where(even, left, right)
-            left, right = rec_ref[3 + ACCEL[c][0], low], rec_ref[3 + ACCEL[c][0], high]
-            near_ref[q, 6 + 3 * c + 2] = jnp.where(even, right, left)
-            far_ref[q, 6 + 3 * c + 2] = jnp.where(even, left, right)
+                both(6 * q + 2 * c + h, w_ref[c, low[q], rows], w_ref[c, high[q], rows])
+                both(12 + 6 * q + 2 * c + h, s_ref[k, low[q], rows], s_ref[k, high[q], rows])
+        left, right = (two_tails(*(rec_ref[3 + k, p] for p in side)) for side in (low, high))
+        both(24 + c, left, right)
 
 
 def plastic_kernel(ahead, s_ref, d_ref, shear_ref, tab_ref, left_ref, grown_ref, *send_ref):
@@ -171,22 +183,25 @@
 
 
 def second_kernel(
-    w_ref, near_ref, far_ref, s_ref, left_ref, shear_ref, mask_ref, v_ref, out_ref, edge_ref, vel
+    w_ref, far_ref, near_ref, s_ref, left_ref, shear_ref, mask_ref, v_ref, out_ref, edge_ref, vel
 ):
-    below, has_left, has_right = mask_ref[0], mask_ref[1], mask_ref[2]
+    below, sides = mask_ref[0], (mask_ref[1], mask_ref[2])
     even = mask_ref[3] > 0.5
 
-    def got(side, q, tile):
-        a, b = near_ref[q, tile], far_ref[q, tile]
+    def got(side, tile):
+        a, b = near_ref[tile], far_ref[tile]
         return jnp.where(even, b, a) if side == 0 else jnp.where(even, a, b)
 
     def got_w(side, q, c):
-        return jnp.concatenate([got(side, q, 2 * c + h) for h in range(2)], axis=0)
+        return jnp.concatenate([got(side, 6 * q + 2 * c + h) for h in range(2)], axis=0)
 
     def got_s(side, q, c):
-        return jnp.concatenate([got(side, q, 6 + 3 * c + h) for h in range(3)], axis=0)
-
-    exists = [jnp.concatenate([m, m], axis=0) for m in (has_left, has_right)]
+        tiles = [got(side, 12 + 6 * q + 2 * c + h) for h in range(2)]
+        tail = got(side, 24 + c)
+        tiles.append(second_tail(tail) if q else tail)
+        return jnp.concatenate([tile * sides[side] for tile in tiles], axis=0)
+
+    exists = [jnp.concatenate([m, m], axis=0) for m in sides]
     for c in range(3):
         ix = ACCEL[c][0]
         m2, m1, p8, p9 = got_s(0, 0, c), got_s(0, 1, c), got_s(1, 0, c), got_s(1, 1, c)
@@ -223,25 +238,28 @@
             edge_ref[3 + k, p] = edge_tile(value)
 
 
-LAST_W, LAST_S, LAST_X, LAST_TILES = 0, 48, 96, 102
-
-
-def last_first_kernel(v_ref, s_ref, rec_ref, mask_ref, w_ref, msg_ref):
+LAST_W, LAST_S, LAST_T, LAST_X, LAST_TILES = 0, 36, 84, 90, 93
+
+
+def last_first_kernel(v_ref, s_ref, rec_ref, mask_ref, unused_ref, w_ref, msg_ref):
     below = mask_ref[0]
     for p in range(PLANES):
         made = partial_update(p, v_ref, s_ref, rec_ref, below)
         for c in range(3):
             w_ref[c, p] = made[c]
             if p < 6:
-                base = LAST_W + 16 * c + (3 * p if p < 4 else 12 + 2 * (p - 4))
-                for h in range(3 if p < 4 else 2):
-                    msg_ref[base + h] = made[c][8 * h : 8 * h + 8]
-            if p < 2:
-                msg_ref[LAST_X + 2 * c + p] = rec_ref[3 + ACCEL[c][0], p]
+                for h in range(2):
+                    msg_ref[LAST_W + 12 * c + 2 * p + h] = made[c][8 * h : 8 * h + 8]
         if p < ADV:
             for k in range(6):
                 for h in range(2):
                     msg_ref[LAST_S + 8 * k + 2 * p + h] = s_ref[k, p, pl.ds(8 * h, 8)]
+    for c in range(3):
+        for q in range(2):
+            tails = (w_ref[c, 2 * q + j, pl.ds(ROWS, TAIL)] for j in range(2))
+            msg_ref[LAST_T + 2 * c + q] = two_tails(*tails)
+        k = 3 + ACCEL[c][0]
+        msg_ref[LAST_X + c] = two_tails(rec_ref[k, 0], rec_ref[k, 1])
 
 
 def last_plastic_kernel(s_ref, d_ref, shear_ref, tab_ref, left_ref, grown_ref):
@@ -271,8 +289,8 @@
 
     for c in range(3):
         ix = ACCEL[c][0]
-        p8 = extended(got_stress(ix, 0), msg_ref[LAST_X + 2 * c])
-        p9 = extended(got_stress(ix, 1), msg_ref[LAST_X + 2 * c + 1])
+        p8 = extended(got_stress(ix, 0), msg_ref[LAST_X + c])
+        p9 = extended(got_stress(ix, 1), second_tail(msg_ref[LAST_X + c]))
         p6 = extended(s_ref[ix, 6], rec_ref[3 + ix, 6])
         p7 = extended(s_ref[ix, 7], rec_ref[3 + ix, 7])
         for p in range(2, 14):
@@ -283,13 +301,15 @@
                 if p == 7:
                     value = value + C8 * p8 - C1 * p9
             elif p < 12:
-                value = got(LAST_W + 16 * c + 3 * (p - 8), 3)
+                r = p - PLANES
+                tail = msg_ref[LAST_T + 2 * c + r // 2]
+                value = extended(got(LAST_W + 12 * c + 2 * r, 2), second_tail(tail) if r % 2 else tail)
                 if p == 8:
                     value = value - C8 * p7 + C1 * p6
                 if p == 9:
                     value = value + C1 * p7
             else:
-                value = got(LAST_W + 16 * c + 12 + 2 * (p - 12), 2)
+                value = got(LAST_W + 12 * c + 2 * (p - PLANES), 2)
             inner = value[:ROWS]
             tail = value[ROWS:] * below if p < 12 else jnp.zeros((TAIL, LANES), F32)
             if p >= PLANES:
@@ -327,6 +347,7 @@
 
 
 VMEM_LIMIT = 16 * 2**20
+HEAVY = 2**34
 
 
 def call(kernel, outs, args, scratch=(), flops=0):
@@ -359,6 +380,18 @@
     upper = lax.ppermute(edge[:, :, :4], "trans", [(i + 1, i) for i in range(count - 1)])
     lower = lax.ppermute(edge[:, :, 4:], "trans", [(i, i + 1) for i in range(count - 1)])
     return jnp.concatenate([upper, lower], axis=2)
+
+
+def all_trade(pairs, count, width):
+    partner = {a: b for a, b in pairs} | {b: a for a, b in pairs}
+    out = []
+    for i in range(count):
+        for t in range(width):
+            if i in partner:
+                out.append((i * width + t, partner[i] * width + t))
+            elif t ^ 1 < width:
+                out.append((i * width + t, i * width + (t ^ 1)))
+    return out
 
 
 def local(velocity, stress, density, shear, normals, directions, inflow):
@@ -377,24 +410,30 @@
     )
     pairs = [(i, i + 1) for i in range(0, count - 1, 2)]
     others = [(i, i + 1) for i in range(1, count - 1, 2)]
-    pairs, others = ([(a, b) for a, b in p] + [(b, a) for a, b in p] for p in (pairs, others))
+    near_swap, far_swap = (all_trade(p, count, lax.axis_size("trans")) for p in (pairs, others))
 
     shape = (PLANES, ROWS, LANES)
     wide = (3, PLANES, EXT, LANES)
     edge_shape = (9, PLANES, TAIL, LANES)
-    (edge,) = call(edges_kernel, [edge_shape], (velocity, stress))
+    edge, velocity, stress = pl.pallas_call(
+        edges_kernel,
+        out_shape=[jax.ShapeDtypeStruct(d, F32) for d in (edge_shape, (3, *shape), (6, *shape))],
+        in_specs=[pl.BlockSpec(memory_space=pltpu.HBM)] * 2,
+        scratch_shapes=[pltpu.SemaphoreType.DMA((9,))],
+        compiler_params=pltpu.CompilerParams(vmem_limit_bytes=VMEM_LIMIT),
+    )(velocity, stress)
     for step in range(STEPS - 1):
         rec = swap_rows(edge)
-        message = (2, 15, 8, LANES)
+        message = (27, 8, LANES)
         w, near, far = call(first_kernel, [wide, message, message], (velocity, stress, rec, masks))
-        far = lax.ppermute(far, "prop", others)
-        near = lax.ppermute(near, "prop", pairs)
+        far = lax.ppermute(far, ("prop", "trans"), far_swap)
+        near = lax.ppermute(near, ("prop", "trans"), near_swap)
         ahead = step == STEPS - 2
         made = call(
             functools.partial(plastic_kernel, ahead),
             [(6, *shape), (12, *shape)] + ([(13, ADV, ROWS, LANES)] if ahead else []),
             (stress, density, shear, table),
-            flops=2**24,
+            flops=HEAVY,
         )
         left, density = made[:2]
         if ahead:
@@ -402,18 +441,18 @@
         velocity, stress, edge = call(
             second_kernel,
             [(3, *shape), (6, *shape), edge_shape],
-            (w, near, far, stress, left, shear, masks),
+            (w, far, near, stress, left, shear, masks),
             scratch=[(3, PLANES + 4, EXT, LANES)],
         )
     rec = swap_rows(edge)
-    w, message = call(
-        last_first_kernel, [wide, (LAST_TILES, 8, LANES)], (velocity, stress, rec, masks)
-    )
-    message = lax.ppermute(message, "prop", [(i + 1, i) for i in range(count - 1)])
     half = (ADV, ROWS, LANES)
     left, grown = call(
-        last_plastic_kernel, [(6, *half), (12, *half)], (stress, density, shear, table), flops=2**23
-    )
+        last_plastic_kernel, [(6, *half), (12, *half)], (stress, density, shear, table), flops=HEAVY
+    )
+    w, message = call(
+        last_first_kernel, [wide, (LAST_TILES, 8, LANES)], (velocity, stress, rec, masks, left)
+    )
+    message = lax.ppermute(message, "prop", [(i + 1, i) for i in range(count - 1)])
     return tuple(
         call(
             last_second_kernel,

time: 64.9 us -> 55.2 us (0.85)
  starting transfers between devices: 20.3 us -> 15 us
  waiting for transfers between devices: 31.7 us -> 27.7 us
  local copies, waits for them, and re-layouts: 3.71 us -> 2.7 us
  Pallas kernels: 7.74 us -> 8.48 us
    ppermute x6, starting transfers between devices: 14.5 us -> 8.01 us  [the longest x3 6.33 us: local(): far = lax.ppermute(far, ('prop', 'trans'), far_swap)]
    ppermute x1, waiting for transfers between devices: 9.82 us -> 6.17 us  [local(): more = lax.ppermute(made[2], 'prop', [(i + 1, i) for i in range(count - 1)])]
    ppermute x1, waiting for transfers between devices: 8.55 us -> 6.71 us  [local(): lax.ppermute(message, 'prop', [(i + 1, i) for i in range(count - 1)])]
    ppermute x4, waiting for transfers between devices: 3.7 us -> 5.13 us  [swap_rows(): return lax.ppermute(edge, 'trans', [(0, 1), (1, 0)])]
    unnamed x18 -> x14, local copies, waits for them, and re-layouts: 3.17 us -> 2.15 us
    ppermute x1, starting transfers between devices: 2.5 us -> 3.46 us  [local(): more = lax.ppermute(made[2], 'prop', [(i + 1, i) for i in range(count - 1)])]
    pallas_call x0 -> x1, Pallas kernels: none -> 0.87 us  [local(): pl.pallas_call(edges_kernel, out_shape=[jax.ShapeDtypeStruct(d, F32) for...]
    pallas_call x13 -> x12, Pallas kernels: 7.74 us -> 7.61 us  [call(): pl.pallas_call(kernel, out_shape=[jax.ShapeDtypeStruct(shape, F32) for sh...]
  transfers between devices with their start and end apart: 12 -> 12, of which waited for: 8 -> 11; matrix products, arithmetic and copies ran while one was open for 1% -> 1% of each run, Pallas kernels for 6% -> 7%
where the time goes in v1:
time: 55.2 us; the launch traced here: 55 us
  waiting for transfers between devices  27.7 us (50%)
  starting transfers between devices  15 us (27%)
  Pallas kernels  8.48 us (15%)
  local copies, waits for them, and re-layouts  2.7 us (5%)
  between operations  0.88 us (2%)
    pallas_call x12, Pallas kernels, call(): pl.pallas_call(kernel, out_shape=[jax.ShapeDtypeStruct(shape, F32) for sh...  7.61 us
    ppermute x1, waiting for transfers between devices, local(): lax.ppermute(message, 'prop', [(i + 1, i) for i in range(count - 1)])  6.71 us
    ppermute x3, waiting for transfers between devices, local(): far = lax.ppermute(far, ('prop', 'trans'), far_swap)  6.49 us
    ppermute x3, starting transfers between devices, local(): far = lax.ppermute(far, ('prop', 'trans'), far_swap)  6.33 us
    ppermute x1, waiting for transfers between devices, local(): more = lax.ppermute(made[2], 'prop', [(i + 1, i) for i in range(count - 1)])  6.17 us
    ppermute x4, waiting for transfers between devices, swap_rows(): return lax.ppermute(edge, 'trans', [(0, 1), (1, 0)])  5.13 us
    ppermute x1, starting transfers between devices, local(): more = lax.ppermute(made[2], 'prop', [(i + 1, i) for i in range(count - 1)])  3.46 us
    ppermute x1, starting transfers between devices, local(): lax.ppermute(message, 'prop', [(i + 1, i) for i in range(count - 1)])  3.29 us
  transfers between devices with their start and end apart: 12, of which 11 were waited for; matrix products, arithmetic and copies ran while one was open for 1% of the time, Pallas kernels for 7%

profile of v1, /device:TPU:14, one launch (start us, length us, event | category | flops | bytes accessed | tf_op | source)
XLA Modules:
  0.0 55.0 jit_solution(13628180303254361977)
XLA Ops:
  0.6 1.0 %copy-done.2 = f32[6,8,16,128]{3,2,1,0:T(8,128)S(1)} copy-done((f32[6,8,16,128]{3,2,1,0:T(8,128)S(1)}, f32[6,8,16,128]{3,2,1,0:T(8,128)}, u32[]{:S(2)}) %copy-start.2) | copy-done | bytes 393240
  1.6 0.9 %copy-done.3 = f32[3,8,16,128]{3,2,1,0:T(8,128)S(1)} copy-done((f32[3,8,16,128]{3,2,1,0:T(8,128)S(1)}, f32[3,8,16,128]{3,2,1,0:T(8,128)}, u32[]{:S(2)}) %copy-start.3) | copy-done | bytes 196632
  2.6 0.9 %shard_map.94 = (f32[9,8,8,128]{3,2,1,0:T(8,128)S(1)}, f32[3,8,16,128]{3,2,1,0:T(8,128)S(1)}, f32[6,8,16,128]{3,2,1,0:T(8,128)S(1)}) custom-call(f32[3,8,16,128]{3,2,1,0:T(8,128)S(1)} %copy-done.3, f32[6,8,16,128]{3,2,1,0:T(8,128)S(1)} %copy-done.2), custom_call_target="tpu_custom_call" | custom-call | tf_op jit(solution)/shard_map/pallas_call | solution.py:418
  4.2 0.9 %collective-permute-done.rec_ref = f32[9,8,8,128]{3,2,1,0:T(8,128)S(1)} collective-permute-done((f32[9,8,8,128]{3,2,1,0:T(8,128)S(1)}, f32[9,8,8,128]{3,2,1,0:T(8,128)S(1)}, u32[]{:S(2)}, u32[]{:S(2)}) %collective-permute-start) | collective-permute-done | bytes 294944 | tf_op jit(solution)/shard_map/ppermute | solution.py:379
  5.5 1.6 %collective-permute-start.1 = (f32[27,8,128]{2,1,0:T(8,128)S(1)}, f32[27,8,128]{2,1,0:T(8,128)S(1)}, u32[]{:S(2)}, u32[]{:S(2)}) collective-permute-start(f32[27,8,128]{2,1,0:T(8,128)S(1)} %get-tuple-element.39), channel_id=1, source_target_pairs={{0,1},{1,0},{2,4},{3,5},{4,2},{5,3},{6,8},{7,9},{8,6},{9,7},{10,12... | collective-permute-start | bytes 331784 | tf_op jit(solution)/shard_map/ppermute | solution.py:429
  7.9 1.0 %shard_map.96 = (f32[6,8,16,128]{3,2,1,0:T(8,128)S(1)}, f32[12,8,16,128]{3,2,1,0:T(8,128)S(1)}) custom-call(f32[6,8,16,128]{3,2,1,0:T(8,128)S(1)} %get-tuple-element.36.s_ref, f32[12,8,16,128]{3,2,1,0:T(8,128)S(1)} %copy-done.4, f32[8,16,128]{2,1,0:T(8,128)S(1)} %copy-done, f32[12,6,8,128]{3,2,1,0:T(8,128)S(1)} %broadcast_in_dim.16.tab_ref), custom_call_target="tpu_custom_call" | custom-call | flops 17179869184 | bytes 1048576 | tf_op jit(solution)/shard_map/pallas_call | solution.py:354
  8.8 3.7 %collective-permute-done.1.far_ref = f32[27,8,128]{2,1,0:T(8,128)S(1)} collective-permute-done((f32[27,8,128]{2,1,0:T(8,128)S(1)}, f32[27,8,128]{2,1,0:T(8,128)S(1)}, u32[]{:S(2)}, u32[]{:S(2)}) %collective-permute-start.1) | collective-permute-done | bytes 110624 | tf_op jit(solution)/shard_map/ppermute | solution.py:429
  13.3 1.6 %collective-permute-done.3.rec_ref = f32[9,8,8,128]{3,2,1,0:T(8,128)S(1)} collective-permute-done((f32[9,8,8,128]{3,2,1,0:T(8,128)S(1)}, f32[9,8,8,128]{3,2,1,0:T(8,128)S(1)}, u32[]{:S(2)}, u32[]{:S(2)}) %collective-permute-start.3) | collective-permute-done | bytes 294944 | tf_op jit(solution)/shard_map/ppermute | solution.py:379
  15.3 2.6 %collective-permute-start.4 = (f32[27,8,128]{2,1,0:T(8,128)S(1)}, f32[27,8,128]{2,1,0:T(8,128)S(1)}, u32[]{:S(2)}, u32[]{:S(2)}) collective-permute-start(f32[27,8,128]{2,1,0:T(8,128)S(1)} %get-tuple-element.46), channel_id=1, source_target_pairs={{0,1},{1,0},{2,4},{3,5},{4,2},{5,3},{6,8},{7,9},{8,6},{9,7},{10,12... | collective-permute-start | bytes 331784 | tf_op jit(solution)/shard_map/ppermute | solution.py:429
  17.9 0.7 %collective-permute-start.5 = (f32[27,8,128]{2,1,0:T(8,128)S(1)}, f32[27,8,128]{2,1,0:T(8,128)S(1)}, u32[]{:S(2)}, u32[]{:S(2)}) collective-permute-start(f32[27,8,128]{2,1,0:T(8,128)S(1)} %get-tuple-element.47), channel_id=1, source_target_pairs={{0,2},{1,3},{2,0},{3,1},{4,6},{5,7},{6,4},{7,5},{8,10},{9,11},{10,... | collective-permute-start | bytes 331784 | tf_op jit(solution)/shard_map/ppermute | solution.py:430
  18.6 1.0 %shard_map.99 = (f32[6,8,16,128]{3,2,1,0:T(8,128)S(1)}, f32[12,8,16,128]{3,2,1,0:T(8,128)S(1)}) custom-call(f32[6,8,16,128]{3,2,1,0:T(8,128)S(1)} %get-tuple-element.43.s_ref, f32[12,8,16,128]{3,2,1,0:T(8,128)S(1)} %get-tuple-element.48.d_ref, f32[8,16,128]{2,1,0:T(8,128)S(1)} %copy-done, f32[12,6,8,128]{3,2,1,0:T(8,128)S(1)} %broadcast_in_dim.16.tab_ref), custom_call_target="tpu_custom_call" | custom-call | flops 17179869184 | bytes 1048576 | tf_op jit(solution)/shard_map/pallas_call | solution.py:354
  19.6 2.8 %collective-permute-done.4.far_ref = f32[27,8,128]{2,1,0:T(8,128)S(1)} collective-permute-done((f32[27,8,128]{2,1,0:T(8,128)S(1)}, f32[27,8,128]{2,1,0:T(8,128)S(1)}, u32[]{:S(2)}, u32[]{:S(2)}) %collective-permute-start.4) | collective-permute-done | bytes 110624 | tf_op jit(solution)/shard_map/ppermute | solution.py:429
  22.4 1.7 %collective-permute-done.5.near_ref = f32[27,8,128]{2,1,0:T(8,128)S(1)} collective-permute-done((f32[27,8,128]{2,1,0:T(8,128)S(1)}, f32[27,8,128]{2,1,0:T(8,128)S(1)}, u32[]{:S(2)}, u32[]{:S(2)}) %collective-permute-start.5) | collective-permute-done | bytes 110624 | tf_op jit(solution)/shard_map/ppermute | solution.py:430
  24.4 1.6 %collective-permute-done.6.rec_ref = f32[9,8,8,128]{3,2,1,0:T(8,128)S(1)} collective-permute-done((f32[9,8,8,128]{3,2,1,0:T(8,128)S(1)}, f32[9,8,8,128]{3,2,1,0:T(8,128)S(1)}, u32[]{:S(2)}, u32[]{:S(2)}) %collective-permute-start.6) | collective-permute-done | bytes 294944 | tf_op jit(solution)/shard_map/ppermute | solution.py:379
  26.4 2.2 %collective-permute-start.7 = (f32[27,8,128]{2,1,0:T(8,128)S(1)}, f32[27,8,128]{2,1,0:T(8,128)S(1)}, u32[]{:S(2)}, u32[]{:S(2)}) collective-permute-start(f32[27,8,128]{2,1,0:T(8,128)S(1)} %get-tuple-element.54), channel_id=1, source_target_pairs={{0,1},{1,0},{2,4},{3,5},{4,2},{5,3},{6,8},{7,9},{8,6},{9,7},{10,12... | collective-permute-start | bytes 331784 | tf_op jit(solution)/shard_map/ppermute | solution.py:429
  29.1 1.0 %shard_map.102 = (f32[6,8,16,128]{3,2,1,0:T(8,128)S(1)}, f32[12,8,16,128]{3,2,1,0:T(8,128)S(1)}, f32[13,4,16,128]{3,2,1,0:T(8,128)S(1)}) custom-call(f32[6,8,16,128]{3,2,1,0:T(8,128)S(1)} %get-tuple-element.51.s_ref, f32[12,8,16,128]{3,2,1,0:T(8,128)S(1)} %get-tuple-element.56.d_ref, f32[8,16,128]{2,1,0:T(8,128)S(1)} %copy-done, ...), custom_call_target="tpu_custom_call" | custom-call | flops 17179869184 | bytes 1048576 | tf_op jit(solution)/shard_map/pallas_call | solution.py:354
  30.0 3.5 %collective-permute-start.11 = (f32[13,4,16,128]{3,2,1,0:T(8,128)S(1)}, f32[13,4,16,128]{3,2,1,0:T(8,128)S(1)}, u32[]{:S(2)}, u32[]{:S(2)}) collective-permute-start(f32[13,4,16,128]{3,2,1,0:T(8,128)S(1)} %get-tuple-element.65), channel_id=1, source_target_pairs={{2,0},{4,2},{6,4},{8,6},{10,8},{12,10},{14,12},{16,14},{18,16},{20... | collective-permute-start | bytes 1277960 | tf_op jit(solution)/shard_map/ppermute | solution.py:440
  33.5 1.2 %collective-permute-done.8.near_ref = f32[27,8,128]{2,1,0:T(8,128)S(1)} collective-permute-done((f32[27,8,128]{2,1,0:T(8,128)S(1)}, f32[27,8,128]{2,1,0:T(8,128)S(1)}, u32[]{:S(2)}, u32[]{:S(2)}) %collective-permute-start.8) | collective-permute-done | bytes 110624 | tf_op jit(solution)/shard_map/ppermute | solution.py:430
  35.0 0.5 shard_map.104
  35.5 1.1 %collective-permute-done.9.rec_ref = f32[9,8,8,128]{3,2,1,0:T(8,128)S(1)} collective-permute-done((f32[9,8,8,128]{3,2,1,0:T(8,128)S(1)}, f32[9,8,8,128]{3,2,1,0:T(8,128)S(1)}, u32[]{:S(2)}, u32[]{:S(2)}) %collective-permute-start.9) | collective-permute-done | bytes 294944 | tf_op jit(solution)/shard_map/ppermute | solution.py:379
  37.0 3.3 %collective-permute-start.10 = (f32[93,8,128]{2,1,0:T(8,128)S(1)}, f32[93,8,128]{2,1,0:T(8,128)S(1)}, u32[]{:S(2)}, u32[]{:S(2)}) collective-permute-start(f32[93,8,128]{2,1,0:T(8,128)S(1)} %get-tuple-element.64), channel_id=1, source_target_pairs={{2,0},{4,2},{6,4},{8,6},{10,8},{12,10},{14,12},{16,14},{18,16},{20... | collective-permute-start | bytes 1142792 | tf_op jit(solution)/shard_map/ppermute | solution.py:455
  40.3 6.2 %collective-permute-done.11.more_ref = f32[13,4,16,128]{3,2,1,0:T(8,128)S(1)} collective-permute-done((f32[13,4,16,128]{3,2,1,0:T(8,128)S(1)}, f32[13,4,16,128]{3,2,1,0:T(8,128)S(1)}, u32[]{:S(2)}, u32[]{:S(2)}) %collective-permute-start.11) | collective-permute-done | bytes 426016 | tf_op jit(solution)/shard_map/ppermute | solution.py:440
  46.5 6.7 %collective-permute-done.10.msg_ref = f32[93,8,128]{2,1,0:T(8,128)S(1)} collective-permute-done((f32[93,8,128]{2,1,0:T(8,128)S(1)}, f32[93,8,128]{2,1,0:T(8,128)S(1)}, u32[]{:S(2)}, u32[]{:S(2)}) %collective-permute-start.10) | collective-permute-done | bytes 380960 | tf_op jit(solution)/shard_map/ppermute | solution.py:455
  53.2 1.8 %shard_map.106 = (f32[3,8,16,128]{3,2,1,0:T(8,128)}, f32[6,8,16,128]{3,2,1,0:T(8,128)}, f32[12,8,16,128]{3,2,1,0:T(8,128)}) custom-call(f32[3,8,24,128]{3,2,1,0:T(8,128)S(1)} %get-tuple-element.63.w_ref, f32[93,8,128]{2,1,0:T(8,128)S(1)} %collective-permute-done.10.msg_ref, f32[13,4,16,128]{3,2,1,0:T(8,128)S(1)} %collective-permute-done.11.more_ref, ...), custom_call_target="tpu_custom_call" | custom-call | bytes 1048576 | tf_op jit(solution)/shard_map/pallas_call | solution.py:354
  (41 shorter events, 5.0 us)
Async XLA Ops:
  0.6 1.0 %copy-start.2 = (f32[6,8,16,128]{3,2,1,0:T(8,128)S(1)}, f32[6,8,16,128]{3,2,1,0:T(8,128)}, u32[]{:S(2)}) copy-start(f32[6,8,16,128]{3,2,1,0:T(8,128)} %s_in.1) | copy-start | bytes 1179652
  1.6 0.9 %copy-start.3 = (f32[3,8,16,128]{3,2,1,0:T(8,128)S(1)}, f32[3,8,16,128]{3,2,1,0:T(8,128)}, u32[]{:S(2)}) copy-start(f32[3,8,16,128]{3,2,1,0:T(8,128)} %v_in.1) | copy-start | bytes 589828
  2.6 1.0 %copy-start.5 = (s32[12,3]{0,1:T(4,128)S(1)}, s32[12,3]{0,1:T(4,128)}, u32[]{:S(2)}) copy-start(s32[12,3]{0,1:T(4,128)} %param.11) | copy-start | bytes 436
  2.6 1.0 %copy-start.6 = (s32[12,3]{0,1:T(4,128)S(1)}, s32[12,3]{0,1:T(4,128)}, u32[]{:S(2)}) copy-start(s32[12,3]{0,1:T(4,128)} %param.12) | copy-start | bytes 436
  3.4 4.2 %copy-start.4 = (f32[12,8,16,128]{3,2,1,0:T(8,128)S(1)}, f32[12,8,16,128]{3,2,1,0:T(8,128)}, u32[]{:S(2)}) copy-start(f32[12,8,16,128]{3,2,1,0:T(8,128)} %d_ref.1) | copy-start | bytes 2359300
  3.5 1.6 %collective-permute-start = (f32[9,8,8,128]{3,2,1,0:T(8,128)S(1)}, f32[9,8,8,128]{3,2,1,0:T(8,128)S(1)}, u32[]{:S(2)}, u32[]{:S(2)}) collective-permute-start(f32[9,8,8,128]{3,2,1,0:T(8,128)S(1)} %get-tuple-element.37), channel_id=1, source_target_pairs={{0,1},{1,0},{2,3},{3,2},{4,5},{5,4},{6,7},{7,6},{8,9},{9,8},{10,11... | collective-permute-start | bytes 884744 | tf_op jit(solution)/shard_map/ppermute | solution.py:379
  5.5 7.1 %collective-permute-start.1 = (f32[27,8,128]{2,1,0:T(8,128)S(1)}, f32[27,8,128]{2,1,0:T(8,128)S(1)}, u32[]{:S(2)}, u32[]{:S(2)}) collective-permute-start(f32[27,8,128]{2,1,0:T(8,128)S(1)} %get-tuple-element.39), channel_id=1, source_target_pairs={{0,1},{1,0},{2,4},{3,5},{4,2},{5,3},{6,8},{7,9},{8,6},{9,7},{10,12... | collective-permute-start | bytes 331784 | tf_op jit(solution)/shard_map/ppermute | solution.py:429
  7.0 0.8 %copy-start = (f32[8,16,128]{2,1,0:T(8,128)S(1)}, f32[8,16,128]{2,1,0:T(8,128)}, u32[]{:S(2)}) copy-start(f32[8,16,128]{2,1,0:T(8,128)} %shear_ref.15) | copy-start | bytes 196612
  7.0 5.9 %collective-permute-start.2 = (f32[27,8,128]{2,1,0:T(8,128)S(1)}, f32[27,8,128]{2,1,0:T(8,128)S(1)}, u32[]{:S(2)}, u32[]{:S(2)}) collective-permute-start(f32[27,8,128]{2,1,0:T(8,128)S(1)} %get-tuple-element.40), channel_id=1, source_target_pairs={{0,2},{1,3},{2,0},{3,1},{4,6},{5,7},{6,4},{7,5},{8,10},{9,11},{10,... | collective-permute-start | bytes 331784 | tf_op jit(solution)/shard_map/ppermute | solution.py:430
  13.3 1.6 %collective-permute-start.3 = (f32[9,8,8,128]{3,2,1,0:T(8,128)S(1)}, f32[9,8,8,128]{3,2,1,0:T(8,128)S(1)}, u32[]{:S(2)}, u32[]{:S(2)}) collective-permute-start(f32[9,8,8,128]{3,2,1,0:T(8,128)S(1)} %get-tuple-element.44), channel_id=1, source_target_pairs={{0,1},{1,0},{2,3},{3,2},{4,5},{5,4},{6,7},{7,6},{8,9},{9,8},{10,11... | collective-permute-start | bytes 884744 | tf_op jit(solution)/shard_map/ppermute | solution.py:379
  15.3 7.1 %collective-permute-start.4 = (f32[27,8,128]{2,1,0:T(8,128)S(1)}, f32[27,8,128]{2,1,0:T(8,128)S(1)}, u32[]{:S(2)}, u32[]{:S(2)}) collective-permute-start(f32[27,8,128]{2,1,0:T(8,128)S(1)} %get-tuple-element.46), channel_id=1, source_target_pairs={{0,1},{1,0},{2,4},{3,5},{4,2},{5,3},{6,8},{7,9},{8,6},{9,7},{10,12... | collective-permute-start | bytes 331784 | tf_op jit(solution)/shard_map/ppermute | solution.py:429
  17.9 6.2 %collective-permute-start.5 = (f32[27,8,128]{2,1,0:T(8,128)S(1)}, f32[27,8,128]{2,1,0:T(8,128)S(1)}, u32[]{:S(2)}, u32[]{:S(2)}) collective-permute-start(f32[27,8,128]{2,1,0:T(8,128)S(1)} %get-tuple-element.47), channel_id=1, source_target_pairs={{0,2},{1,3},{2,0},{3,1},{4,6},{5,7},{6,4},{7,5},{8,10},{9,11},{10,... | collective-permute-start | bytes 331784 | tf_op jit(solution)/shard_map/ppermute | solution.py:430
  24.4 1.6 %collective-permute-start.6 = (f32[9,8,8,128]{3,2,1,0:T(8,128)S(1)}, f32[9,8,8,128]{3,2,1,0:T(8,128)S(1)}, u32[]{:S(2)}, u32[]{:S(2)}) collective-permute-start(f32[9,8,8,128]{3,2,1,0:T(8,128)S(1)} %get-tuple-element.52), channel_id=1, source_target_pairs={{0,1},{1,0},{2,3},{3,2},{4,5},{5,4},{6,7},{7,6},{8,9},{9,8},{10,11... | collective-permute-start | bytes 884744 | tf_op jit(solution)/shard_map/ppermute | solution.py:379
  26.4 7.1 %collective-permute-start.7 = (f32[27,8,128]{2,1,0:T(8,128)S(1)}, f32[27,8,128]{2,1,0:T(8,128)S(1)}, u32[]{:S(2)}, u32[]{:S(2)}) collective-permute-start(f32[27,8,128]{2,1,0:T(8,128)S(1)} %get-tuple-element.54), channel_id=1, source_target_pairs={{0,1},{1,0},{2,4},{3,5},{4,2},{5,3},{6,8},{7,9},{8,6},{9,7},{10,12... | collective-permute-start | bytes 331784 | tf_op jit(solution)/shard_map/ppermute | solution.py:429
  28.6 6.1 %collective-permute-start.8 = (f32[27,8,128]{2,1,0:T(8,128)S(1)}, f32[27,8,128]{2,1,0:T(8,128)S(1)}, u32[]{:S(2)}, u32[]{:S(2)}) collective-permute-start(f32[27,8,128]{2,1,0:T(8,128)S(1)} %get-tuple-element.55), channel_id=1, source_target_pairs={{0,2},{1,3},{2,0},{3,1},{4,6},{5,7},{6,4},{7,5},{8,10},{9,11},{10,... | collective-permute-start | bytes 331784 | tf_op jit(solution)/shard_map/ppermute | solution.py:430
  30.0 16.4 %collective-permute-start.11 = (f32[13,4,16,128]{3,2,1,0:T(8,128)S(1)}, f32[13,4,16,128]{3,2,1,0:T(8,128)S(1)}, u32[]{:S(2)}, u32[]{:S(2)}) collective-permute-start(f32[13,4,16,128]{3,2,1,0:T(8,128)S(1)} %get-tuple-element.65), channel_id=1, source_target_pairs={{2,0},{4,2},{6,4},{8,6},{10,8},{12,10},{14,12},{16,14},{18,16},{20... | collective-permute-start | bytes 1277960 | tf_op jit(solution)/shard_map/ppermute | solution.py:440
  35.0 1.6 %collective-permute-start.9 = (f32[9,8,8,128]{3,2,1,0:T(8,128)S(1)}, f32[9,8,8,128]{3,2,1,0:T(8,128)S(1)}, u32[]{:S(2)}, u32[]{:S(2)}) collective-permute-start(f32[9,8,8,128]{3,2,1,0:T(8,128)S(1)} %get-tuple-element.60), channel_id=1, source_target_pairs={{0,1},{1,0},{2,3},{3,2},{4,5},{5,4},{6,7},{7,6},{8,9},{9,8},{10,11... | collective-permute-start | bytes 884744 | tf_op jit(solution)/shard_map/ppermute | solution.py:379
  35.5 17.6 %copy-start.1 = (f32[21,4,16,128]{3,2,1,0:T(8,128)S(1)}, f32[21,4,16,128]{3,2,1,0:T(8,128)}, u32[]{:S(2)}) copy-start(f32[21,4,16,128]{3,2,1,0:T(8,128)} %inflow_ref.1) | copy-start | bytes 2064388
  37.0 16.2 %collective-permute-start.10 = (f32[93,8,128]{2,1,0:T(8,128)S(1)}, f32[93,8,128]{2,1,0:T(8,128)S(1)}, u32[]{:S(2)}, u32[]{:S(2)}) collective-permute-start(f32[93,8,128]{2,1,0:T(8,128)S(1)} %get-tuple-element.64), channel_id=1, source_target_pairs={{2,0},{4,2},{6,4},{8,6},{10,8},{12,10},{14,12},{16,14},{18,16},{20... | collective-permute-start | bytes 1142792 | tf_op jit(solution)/shard_map/ppermute | solution.py:455

commit v2 on v1

--- a/solution.py
+++ b/solution.py
@@ -54,13 +54,26 @@
     return jnp.where(row < 4, plane[:TAIL], plane[ROWS - TAIL :])
 
 
-def two_tails(a, b):
+def pack_tails(tails, per, mask_ref):
     row = lax.broadcasted_iota(jnp.int32, (TAIL, LANES), 0)
-    return jnp.where((row < 2) | (row >= 6), a, pltpu.roll(b, 4, 0))
-
-
-def second_tail(tile):
-    return pltpu.roll(tile, 4, 0)
+    if per == 4:
+        pair = row // 2
+        place = jnp.where(mask_ref[4] > 0.5, pair, (pair + 1) % 4)
+    else:
+        place = jnp.where((row < 2) | (row >= 6), 0, 1)
+    tiles = []
+    for first in range(0, len(tails), per):
+        tile = tails[first]
+        for j, tail in enumerate(tails[first : first + per]):
+            if j:
+                tile = jnp.where(place == j, pltpu.roll(tail, TAIL // per * j, 0), tile)
+        tiles.append(tile)
+    return tiles
+
+
+def unpack_tail(tile_at, index, per):
+    tile, j = tile_at(index // per), index % per
+    return pltpu.roll(tile, TAIL - TAIL // per * j, 0) if j else tile
 
 
 def plastic_parts(stress, densities, shear, tab_ref):
@@ -144,7 +157,7 @@
     return out
 
 
-def first_kernel(v_ref, s_ref, rec_ref, mask_ref, w_ref, near_ref, far_ref):
+def first_kernel(per, v_ref, s_ref, rec_ref, mask_ref, w_ref, near_ref, far_ref):
     below = mask_ref[0]
     even = mask_ref[3] > 0.5
     for p in range(PLANES):
@@ -163,8 +176,12 @@
                 rows = pl.ds(8 * h, 8)
                 both(6 * q + 2 * c + h, w_ref[c, low[q], rows], w_ref[c, high[q], rows])
                 both(12 + 6 * q + 2 * c + h, s_ref[k, low[q], rows], s_ref[k, high[q], rows])
-        left, right = (two_tails(*(rec_ref[3 + k, p] for p in side)) for side in (low, high))
-        both(24 + c, left, right)
+    packed = [
+        pack_tails([rec_ref[3 + ACCEL[c][0], p] for c in range(3) for p in side], per, mask_ref)
+        for side in (low, high)
+    ]
+    for tile, (left, right) in enumerate(zip(*packed)):
+        both(24 + tile, left, right)
 
 
 def plastic_kernel(ahead, s_ref, d_ref, shear_ref, tab_ref, left_ref, grown_ref, *send_ref):
@@ -183,7 +200,7 @@
 
 
 def second_kernel(
-    w_ref, far_ref, near_ref, s_ref, left_ref, shear_ref, mask_ref, v_ref, out_ref, edge_ref, vel
+    per, w_ref, far_ref, near_ref, s_ref, left_ref, shear_ref, mask_ref, v_ref, out_ref, edge_ref, vel
 ):
     below, sides = mask_ref[0], (mask_ref[1], mask_ref[2])
     even = mask_ref[3] > 0.5
@@ -197,8 +214,7 @@
 
     def got_s(side, q, c):
         tiles = [got(side, 12 + 6 * q + 2 * c + h) for h in range(2)]
-        tail = got(side, 24 + c)
-        tiles.append(second_tail(tail) if q else tail)
+        tiles.append(unpack_tail(lambda tile: got(side, 24 + tile), 2 * c + q, per))
         return jnp.concatenate([tile * sides[side] for tile in tiles], axis=0)
 
     exists = [jnp.concatenate([m, m], axis=0) for m in sides]
@@ -238,10 +254,10 @@
             edge_ref[3 + k, p] = edge_tile(value)
 
 
-LAST_W, LAST_S, LAST_T, LAST_X, LAST_TILES = 0, 36, 84, 90, 93
-
-
-def last_first_kernel(v_ref, s_ref, rec_ref, mask_ref, unused_ref, w_ref, msg_ref):
+LAST_W, LAST_S, LAST_T, LAST_TAILS = 0, 36, 84, 18
+
+
+def last_first_kernel(per, v_ref, s_ref, rec_ref, mask_ref, unused_ref, w_ref, msg_ref):
     below = mask_ref[0]
     for p in range(PLANES):
         made = partial_update(p, v_ref, s_ref, rec_ref, below)
@@ -254,12 +270,10 @@
             for k in range(6):
                 for h in range(2):
                     msg_ref[LAST_S + 8 * k + 2 * p + h] = s_ref[k, p, pl.ds(8 * h, 8)]
-    for c in range(3):
-        for q in range(2):
-            tails = (w_ref[c, 2 * q + j, pl.ds(ROWS, TAIL)] for j in range(2))
-            msg_ref[LAST_T + 2 * c + q] = two_tails(*tails)
-        k = 3 + ACCEL[c][0]
-        msg_ref[LAST_X + c] = two_tails(rec_ref[k, 0], rec_ref[k, 1])
+    tails = [w_ref[c, p, pl.ds(ROWS, TAIL)] for c in range(3) for p in range(ADV)]
+    tails += [rec_ref[3 + ACCEL[c][0], p] for c in range(3) for p in range(2)]
+    for tile, packed in enumerate(pack_tails(tails, per, mask_ref)):
+        msg_ref[LAST_T + tile] = packed
 
 
 def last_plastic_kernel(s_ref, d_ref, shear_ref, tab_ref, left_ref, grown_ref):
@@ -274,9 +288,16 @@
 
 
 def last_second_kernel(
-    w_ref, msg_ref, more_ref, s_ref, rec_ref, left_ref, grown_ref, shear_ref, tab_ref, mask_ref, inflow_ref,
-    v_ref, out_ref, d_ref, vel,
+    per, w_ref, msg_ref, more_ref, s_ref, rec_ref, left_ref, grown_ref, shear_ref, tab_ref, mask_ref, inflow_ref,
+    v_out, s_out, d_out, vel, v_ref, out_ref, d_ref, sems,
 ):
+    copies = []
+
+    def write(source, target):
+        copies.append(pltpu.make_async_copy(source, target, sems.at[len(copies)]))
+        copies[-1].start()
+
+    write(grown_ref, d_out.at[:, pl.ds(0, ADV)])
     below = mask_ref[0]
     here = jnp.concatenate([mask_ref[2]] * 2, axis=0)
     inside = here > 0.5
@@ -284,13 +305,16 @@
     def got(base, count):
         return jnp.concatenate([msg_ref[base + h] for h in range(count)], axis=0)
 
+    def got_tail(index):
+        return unpack_tail(lambda tile: msg_ref[LAST_T + tile], index, per)
+
     def got_stress(k, p):
         return got(LAST_S + 8 * k + 2 * p, 2)
 
     for c in range(3):
         ix = ACCEL[c][0]
-        p8 = extended(got_stress(ix, 0), msg_ref[LAST_X + c])
-        p9 = extended(got_stress(ix, 1), second_tail(msg_ref[LAST_X + c]))
+        p8 = extended(got_stress(ix, 0), got_tail(12 + 2 * c))
+        p9 = extended(got_stress(ix, 1), got_tail(12 + 2 * c + 1))
         p6 = extended(s_ref[ix, 6], rec_ref[3 + ix, 6])
         p7 = extended(s_ref[ix, 7], rec_ref[3 + ix, 7])
         for p in range(2, 14):
@@ -302,8 +326,7 @@
                     value = value + C8 * p8 - C1 * p9
             elif p < 12:
                 r = p - PLANES
-                tail = msg_ref[LAST_T + 2 * c + r // 2]
-                value = extended(got(LAST_W + 12 * c + 2 * r, 2), second_tail(tail) if r % 2 else tail)
+                value = extended(got(LAST_W + 12 * c + 2 * r, 2), got_tail(4 * c + r))
                 if p == 8:
                     value = value - C8 * p7 + C1 * p6
                 if p == 9:
@@ -319,11 +342,11 @@
                 if p >= PLANES:
                     inner = jnp.where(inside, inner, inflow_ref[c, p - PLANES])
                 v_ref[c, p - ADV] = inner
+    write(v_ref, v_out)
     for q in range(PLANES):
         p = q + ADV
         if p < PLANES:
             left = [left_ref[k, q] for k in range(6)]
-            grown = [grown_ref[s, q] for s in range(12)]
             shear = shear_ref[p]
         else:
             r = p - PLANES
@@ -339,11 +362,13 @@
             if p >= PLANES:
                 value = jnp.where(inside, value, inflow_ref[3 + k, p - PLANES])
             out_ref[k, q] = value
-        for s in range(12):
-            value = grown[s]
-            if p >= PLANES:
-                value = jnp.where(inside, value, inflow_ref[9 + s, p - PLANES])
-            d_ref[s, q] = value
+        write(out_ref.at[:, q], s_out.at[:, q])
+        if p >= PLANES:
+            for s in range(12):
+                d_ref[s, p - PLANES] = jnp.where(inside, grown[s], inflow_ref[9 + s, p - PLANES])
+            write(d_ref.at[:, p - PLANES], d_out.at[:, q])
+    for copy in copies:
+        copy.wait()
 
 
 VMEM_LIMIT = 16 * 2**20
@@ -406,26 +431,28 @@
             full * (at > 0).astype(F32),
             full * (at < count - 1).astype(F32),
             full * (at % 2 == 0).astype(F32),
+            full * (side < lax.axis_size("trans") - 1).astype(F32),
         ]
     )
     pairs = [(i, i + 1) for i in range(0, count - 1, 2)]
     others = [(i, i + 1) for i in range(1, count - 1, 2)]
     near_swap, far_swap = (all_trade(p, count, lax.axis_size("trans")) for p in (pairs, others))
 
+    per = 4 if lax.axis_size("trans") == 2 else 2
     shape = (PLANES, ROWS, LANES)
     wide = (3, PLANES, EXT, LANES)
     edge_shape = (9, PLANES, TAIL, LANES)
     edge, velocity, stress = pl.pallas_call(
         edges_kernel,
-        out_shape=[jax.ShapeDtypeStruct(d, F32) for d in (edge_shape, (3, *shape), (6, *shape))],
+        out_shape=[pltpu.VMEM(d, F32) for d in (edge_shape, (3, *shape), (6, *shape))],
         in_specs=[pl.BlockSpec(memory_space=pltpu.HBM)] * 2,
         scratch_shapes=[pltpu.SemaphoreType.DMA((9,))],
-        compiler_params=pltpu.CompilerParams(vmem_limit_bytes=VMEM_LIMIT),
+        compiler_params=pltpu.CompilerParams(vmem_limit_bytes=60 * 2**20),
     )(velocity, stress)
     for step in range(STEPS - 1):
         rec = swap_rows(edge)
-        message = (27, 8, LANES)
-        w, near, far = call(first_kernel, [wide, message, message], (velocity, stress, rec, masks))
+        message = (24 + -(-6 // per), 8, LANES)
+        w, near, far = call(functools.partial(first_kernel, per), [wide, message, message], (velocity, stress, rec, masks))
         far = lax.ppermute(far, ("prop", "trans"), far_swap)
         near = lax.ppermute(near, ("prop", "trans"), near_swap)
         ahead = step == STEPS - 2
@@ -439,7 +466,7 @@
         if ahead:
             more = lax.ppermute(made[2], "prop", [(i + 1, i) for i in range(count - 1)])
         velocity, stress, edge = call(
-            second_kernel,
+            functools.partial(second_kernel, per),
             [(3, *shape), (6, *shape), edge_shape],
             (w, far, near, stress, left, shear, masks),
             scratch=[(3, PLANES + 4, EXT, LANES)],
@@ -450,16 +477,24 @@
         last_plastic_kernel, [(6, *half), (12, *half)], (stress, density, shear, table), flops=HEAVY
     )
     w, message = call(
-        last_first_kernel, [wide, (LAST_TILES, 8, LANES)], (velocity, stress, rec, masks, left)
+        functools.partial(last_first_kernel, per),
+        [wide, (LAST_T + -(-LAST_TAILS // per), 8, LANES)],
+        (velocity, stress, rec, masks, left)
     )
     message = lax.ppermute(message, "prop", [(i + 1, i) for i in range(count - 1)])
+    shapes = [(3, *shape), (6, *shape), (12, *shape)]
     return tuple(
-        call(
-            last_second_kernel,
-            [(3, *shape), (6, *shape), (12, *shape)],
-            (w, message, more, stress, rec, left, grown, shear, table, masks, inflow),
-            scratch=[(3, PLANES + 4, EXT, LANES)],
-        )
+        pl.pallas_call(
+            functools.partial(last_second_kernel, per),
+            out_shape=[jax.ShapeDtypeStruct(d, F32) for d in shapes],
+            out_specs=[pl.BlockSpec(memory_space=pl.ANY)] * 3,
+            scratch_shapes=[
+                pltpu.VMEM((3, PLANES + 4, EXT, LANES), F32),
+                *(pltpu.VMEM(d, F32) for d in (*shapes[:2], (12, *half))),
+                pltpu.SemaphoreType.DMA((2 + PLANES + ADV,)),
+            ],
+            compiler_params=pltpu.CompilerParams(vmem_limit_bytes=VMEM_LIMIT),
+        )(w, message, more, stress, rec, left, grown, shear, table, masks, inflow)
     )
 
 

time: 55.2 us -> 52.8 us (0.957)
  local copies, waits for them, and re-layouts: 2.7 us -> 0.56 us
    pallas_call x1 -> x2, Pallas kernels: 0.87 us -> 2.79 us  [the longest x1 1.6 us: local(): pl.pallas_call(functools.partial(last_second_kernel, per), out_shape=[jax...]
    unnamed x14, local copies, waits for them, and re-layouts: 2.15 us -> 0.31 us
    pallas_call x12 -> x11, Pallas kernels: 7.61 us -> 5.9 us  [call(): pl.pallas_call(kernel, out_shape=[jax.ShapeDtypeStruct(shape, F32) for sh...]
  transfers between devices with their start and end apart: 12 -> 12, of which waited for: 11 -> 11; matrix products, arithmetic and copies ran while one was open for 1% -> 1% of each run, Pallas kernels for 7% -> 8%
where the time goes in v2:
time: 52.8 us; the launch traced here: 52.5 us
  waiting for transfers between devices  27.2 us (52%)
  starting transfers between devices  15.1 us (29%)
  Pallas kernels  8.69 us (16%)
  between operations  0.91 us (2%)
  local copies, waits for them, and re-layouts  0.56 us (1%)
    ppermute x1, waiting for transfers between devices, local(): more = lax.ppermute(made[2], 'prop', [(i + 1, i) for i in range(count - 1)])  6.43 us
    ppermute x1, waiting for transfers between devices, local(): lax.ppermute(message, 'prop', [(i + 1, i) for i in range(count - 1)])  6.36 us
    ppermute x3, starting transfers between devices, local(): far = lax.ppermute(far, ('prop', 'trans'), far_swap)  6.33 us
    ppermute x3, waiting for transfers between devices, local(): far = lax.ppermute(far, ('prop', 'trans'), far_swap)  6.29 us
    pallas_call x11, Pallas kernels, call(): pl.pallas_call(kernel, out_shape=[jax.ShapeDtypeStruct(shape, F32) for sh...  5.9 us
    ppermute x4, waiting for transfers between devices, swap_rows(): return lax.ppermute(edge, 'trans', [(0, 1), (1, 0)])  5.4 us
    ppermute x1, starting transfers between devices, local(): more = lax.ppermute(made[2], 'prop', [(i + 1, i) for i in range(count - 1)])  3.46 us
    ppermute x1, starting transfers between devices, local(): lax.ppermute(message, 'prop', [(i + 1, i) for i in range(count - 1)])  3.37 us
  transfers between devices with their start and end apart: 12, of which 11 were waited for; matrix products, arithmetic and copies ran while one was open for 1% of the time, Pallas kernels for 8%

profile of v2, /device:TPU:14, one launch (start us, length us, event | category | flops | bytes accessed | tf_op | source)
XLA Modules:
  0.0 52.5 jit_solution(6384483001777975514)
XLA Ops:
  0.7 1.2 %shard_map.94 = (f32[9,8,8,128]{3,2,1,0:T(8,128)S(1)}, f32[3,8,16,128]{3,2,1,0:T(8,128)S(1)}, f32[6,8,16,128]{3,2,1,0:T(8,128)S(1)}) custom-call(f32[3,8,16,128]{3,2,1,0:T(8,128)} %v_in.1, f32[6,8,16,128]{3,2,1,0:T(8,128)} %s_in.1), custom_call_target="tpu_custom_call" | custom-call | tf_op jit(solution)/shard_map/pallas_call | solution.py:445
  2.3 1.2 %collective-permute-done.rec_ref = f32[9,8,8,128]{3,2,1,0:T(8,128)S(1)} collective-permute-done((f32[9,8,8,128]{3,2,1,0:T(8,128)S(1)}, f32[9,8,8,128]{3,2,1,0:T(8,128)S(1)}, u32[]{:S(2)}, u32[]{:S(2)}) %collective-permute-start) | collective-permute-done | bytes 294944 | tf_op jit(solution)/shard_map/ppermute | solution.py:404
  3.9 1.6 %collective-permute-start.1 = (f32[26,8,128]{2,1,0:T(8,128)S(1)}, f32[26,8,128]{2,1,0:T(8,128)S(1)}, u32[]{:S(2)}, u32[]{:S(2)}) collective-permute-start(f32[26,8,128]{2,1,0:T(8,128)S(1)} %get-tuple-element.39), channel_id=1, source_target_pairs={{0,1},{1,0},{2,4},{3,5},{4,2},{5,3},{6,8},{7,9},{8,6},{9,7},{10,12... | collective-permute-start | bytes 319496 | tf_op jit(solution)/shard_map/ppermute | solution.py:456
  5.4 0.5 collective-permute-start.2
  6.3 1.0 %shard_map.96 = (f32[6,8,16,128]{3,2,1,0:T(8,128)S(1)}, f32[12,8,16,128]{3,2,1,0:T(8,128)S(1)}) custom-call(f32[6,8,16,128]{3,2,1,0:T(8,128)S(1)} %get-tuple-element.36.s_ref, f32[12,8,16,128]{3,2,1,0:T(8,128)S(1)} %copy-done.2, f32[8,16,128]{2,1,0:T(8,128)S(1)} %copy-done, f32[12,6,8,128]{3,2,1,0:T(8,128)S(1)} %broadcast_in_dim.16.tab_ref), custom_call_target="tpu_custom_call" | custom-call | flops 17179869184 | bytes 1048576 | tf_op jit(solution)/shard_map/pallas_call | solution.py:379
  7.3 3.6 %collective-permute-done.1.far_ref = f32[26,8,128]{2,1,0:T(8,128)S(1)} collective-permute-done((f32[26,8,128]{2,1,0:T(8,128)S(1)}, f32[26,8,128]{2,1,0:T(8,128)S(1)}, u32[]{:S(2)}, u32[]{:S(2)}) %collective-permute-start.1) | collective-permute-done | bytes 106528 | tf_op jit(solution)/shard_map/ppermute | solution.py:456
  11.6 1.6 %collective-permute-done.3.rec_ref = f32[9,8,8,128]{3,2,1,0:T(8,128)S(1)} collective-permute-done((f32[9,8,8,128]{3,2,1,0:T(8,128)S(1)}, f32[9,8,8,128]{3,2,1,0:T(8,128)S(1)}, u32[]{:S(2)}, u32[]{:S(2)}) %collective-permute-start.3) | collective-permute-done | bytes 294944 | tf_op jit(solution)/shard_map/ppermute | solution.py:404
  13.5 2.6 %collective-permute-start.4 = (f32[26,8,128]{2,1,0:T(8,128)S(1)}, f32[26,8,128]{2,1,0:T(8,128)S(1)}, u32[]{:S(2)}, u32[]{:S(2)}) collective-permute-start(f32[26,8,128]{2,1,0:T(8,128)S(1)} %get-tuple-element.46), channel_id=1, source_target_pairs={{0,1},{1,0},{2,4},{3,5},{4,2},{5,3},{6,8},{7,9},{8,6},{9,7},{10,12... | collective-permute-start | bytes 319496 | tf_op jit(solution)/shard_map/ppermute | solution.py:456
  16.1 0.7 %collective-permute-start.5 = (f32[26,8,128]{2,1,0:T(8,128)S(1)}, f32[26,8,128]{2,1,0:T(8,128)S(1)}, u32[]{:S(2)}, u32[]{:S(2)}) collective-permute-start(f32[26,8,128]{2,1,0:T(8,128)S(1)} %get-tuple-element.47), channel_id=1, source_target_pairs={{0,2},{1,3},{2,0},{3,1},{4,6},{5,7},{6,4},{7,5},{8,10},{9,11},{10,... | collective-permute-start | bytes 319496 | tf_op jit(solution)/shard_map/ppermute | solution.py:457
  16.8 1.0 %shard_map.99 = (f32[6,8,16,128]{3,2,1,0:T(8,128)S(1)}, f32[12,8,16,128]{3,2,1,0:T(8,128)S(1)}) custom-call(f32[6,8,16,128]{3,2,1,0:T(8,128)S(1)} %get-tuple-element.43.s_ref, f32[12,8,16,128]{3,2,1,0:T(8,128)S(1)} %get-tuple-element.48.d_ref, f32[8,16,128]{2,1,0:T(8,128)S(1)} %copy-done, f32[12,6,8,128]{3,2,1,0:T(8,128)S(1)} %broadcast_in_dim.16.tab_ref), custom_call_target="tpu_custom_call" | custom-call | flops 17179869184 | bytes 1048576 | tf_op jit(solution)/shard_map/pallas_call | solution.py:379
  17.8 2.7 %collective-permute-done.4.far_ref = f32[26,8,128]{2,1,0:T(8,128)S(1)} collective-permute-done((f32[26,8,128]{2,1,0:T(8,128)S(1)}, f32[26,8,128]{2,1,0:T(8,128)S(1)}, u32[]{:S(2)}, u32[]{:S(2)}) %collective-permute-start.4) | collective-permute-done | bytes 106528 | tf_op jit(solution)/shard_map/ppermute | solution.py:456
  20.5 1.6 %collective-permute-done.5.near_ref = f32[26,8,128]{2,1,0:T(8,128)S(1)} collective-permute-done((f32[26,8,128]{2,1,0:T(8,128)S(1)}, f32[26,8,128]{2,1,0:T(8,128)S(1)}, u32[]{:S(2)}, u32[]{:S(2)}) %collective-permute-start.5) | collective-permute-done | bytes 106528 | tf_op jit(solution)/shard_map/ppermute | solution.py:457
  22.5 1.6 %collective-permute-done.6.rec_ref = f32[9,8,8,128]{3,2,1,0:T(8,128)S(1)} collective-permute-done((f32[9,8,8,128]{3,2,1,0:T(8,128)S(1)}, f32[9,8,8,128]{3,2,1,0:T(8,128)S(1)}, u32[]{:S(2)}, u32[]{:S(2)}) %collective-permute-start.6) | collective-permute-done | bytes 294944 | tf_op jit(solution)/shard_map/ppermute | solution.py:404
  24.5 2.2 %collective-permute-start.7 = (f32[26,8,128]{2,1,0:T(8,128)S(1)}, f32[26,8,128]{2,1,0:T(8,128)S(1)}, u32[]{:S(2)}, u32[]{:S(2)}) collective-permute-start(f32[26,8,128]{2,1,0:T(8,128)S(1)} %get-tuple-element.54), channel_id=1, source_target_pairs={{0,1},{1,0},{2,4},{3,5},{4,2},{5,3},{6,8},{7,9},{8,6},{9,7},{10,12... | collective-permute-start | bytes 319496 | tf_op jit(solution)/shard_map/ppermute | solution.py:456
  26.7 0.5 collective-permute-start.8
  27.1 1.0 %shard_map.102 = (f32[6,8,16,128]{3,2,1,0:T(8,128)S(1)}, f32[12,8,16,128]{3,2,1,0:T(8,128)S(1)}, f32[13,4,16,128]{3,2,1,0:T(8,128)S(1)}) custom-call(f32[6,8,16,128]{3,2,1,0:T(8,128)S(1)} %get-tuple-element.51.s_ref, f32[12,8,16,128]{3,2,1,0:T(8,128)S(1)} %get-tuple-element.56.d_ref, f32[8,16,128]{2,1,0:T(8,128)S(1)} %copy-done, ...), custom_call_target="tpu_custom_call" | custom-call | flops 17179869184 | bytes 1048576 | tf_op jit(solution)/shard_map/pallas_call | solution.py:379
  28.1 3.5 %collective-permute-start.11 = (f32[13,4,16,128]{3,2,1,0:T(8,128)S(1)}, f32[13,4,16,128]{3,2,1,0:T(8,128)S(1)}, u32[]{:S(2)}, u32[]{:S(2)}) collective-permute-start(f32[13,4,16,128]{3,2,1,0:T(8,128)S(1)} %get-tuple-element.65), channel_id=1, source_target_pairs={{2,0},{4,2},{6,4},{8,6},{10,8},{12,10},{14,12},{16,14},{18,16},{20... | collective-permute-start | bytes 1277960 | tf_op jit(solution)/shard_map/ppermute | solution.py:467
  31.6 0.8 %collective-permute-done.8.near_ref = f32[26,8,128]{2,1,0:T(8,128)S(1)} collective-permute-done((f32[26,8,128]{2,1,0:T(8,128)S(1)}, f32[26,8,128]{2,1,0:T(8,128)S(1)}, u32[]{:S(2)}, u32[]{:S(2)}) %collective-permute-start.8) | collective-permute-done | bytes 106528 | tf_op jit(solution)/shard_map/ppermute | solution.py:457
  32.8 0.5 shard_map.104
  33.3 1.1 %collective-permute-done.9.rec_ref = f32[9,8,8,128]{3,2,1,0:T(8,128)S(1)} collective-permute-done((f32[9,8,8,128]{3,2,1,0:T(8,128)S(1)}, f32[9,8,8,128]{3,2,1,0:T(8,128)S(1)}, u32[]{:S(2)}, u32[]{:S(2)}) %collective-permute-start.9) | collective-permute-done | bytes 294944 | tf_op jit(solution)/shard_map/ppermute | solution.py:404
  34.8 3.4 %collective-permute-start.10 = (f32[89,8,128]{2,1,0:T(8,128)S(1)}, f32[89,8,128]{2,1,0:T(8,128)S(1)}, u32[]{:S(2)}, u32[]{:S(2)}) collective-permute-start(f32[89,8,128]{2,1,0:T(8,128)S(1)} %get-tuple-element.64), channel_id=1, source_target_pairs={{2,0},{4,2},{6,4},{8,6},{10,8},{12,10},{14,12},{16,14},{18,16},{20... | collective-permute-start | bytes 1093640 | tf_op jit(solution)/shard_map/ppermute | solution.py:484
  38.1 6.4 %collective-permute-done.11.more_ref = f32[13,4,16,128]{3,2,1,0:T(8,128)S(1)} collective-permute-done((f32[13,4,16,128]{3,2,1,0:T(8,128)S(1)}, f32[13,4,16,128]{3,2,1,0:T(8,128)S(1)}, u32[]{:S(2)}, u32[]{:S(2)}) %collective-permute-start.11) | collective-permute-done | bytes 426016 | tf_op jit(solution)/shard_map/ppermute | solution.py:467
  44.6 6.4 %collective-permute-done.10.msg_ref = f32[89,8,128]{2,1,0:T(8,128)S(1)} collective-permute-done((f32[89,8,128]{2,1,0:T(8,128)S(1)}, f32[89,8,128]{2,1,0:T(8,128)S(1)}, u32[]{:S(2)}, u32[]{:S(2)}) %collective-permute-start.10) | collective-permute-done | bytes 364576 | tf_op jit(solution)/shard_map/ppermute | solution.py:484
  50.9 1.6 %shard_map.106 = (f32[3,8,16,128]{3,2,1,0:T(8,128)}, f32[6,8,16,128]{3,2,1,0:T(8,128)}, f32[12,8,16,128]{3,2,1,0:T(8,128)}) custom-call(f32[3,8,24,128]{3,2,1,0:T(8,128)S(1)} %get-tuple-element.63.w_ref, f32[89,8,128]{2,1,0:T(8,128)S(1)} %collective-permute-done.10.msg_ref, f32[13,4,16,128]{3,2,1,0:T(8,128)S(1)} %collective-permute-done.11.more_ref, ...), custom_call_target="tpu_custom_call" | custom-call | tf_op jit(solution)/shard_map/pallas_call | solution.py:487
  (37 shorter events, 3.7 us)
Async XLA Ops:
  0.6 1.3 %copy-start.3 = (s32[12,3]{0,1:T(4,128)S(1)}, s32[12,3]{0,1:T(4,128)}, u32[]{:S(2)}) copy-start(s32[12,3]{0,1:T(4,128)} %param.11) | copy-start | bytes 436
  0.6 1.3 %copy-start.4 = (s32[12,3]{0,1:T(4,128)S(1)}, s32[12,3]{0,1:T(4,128)}, u32[]{:S(2)}) copy-start(s32[12,3]{0,1:T(4,128)} %param.12) | copy-start | bytes 436
  1.8 4.2 %copy-start.2 = (f32[12,8,16,128]{3,2,1,0:T(8,128)S(1)}, f32[12,8,16,128]{3,2,1,0:T(8,128)}, u32[]{:S(2)}) copy-start(f32[12,8,16,128]{3,2,1,0:T(8,128)} %d_ref.1) | copy-start | bytes 2359300
  1.9 1.6 %collective-permute-start = (f32[9,8,8,128]{3,2,1,0:T(8,128)S(1)}, f32[9,8,8,128]{3,2,1,0:T(8,128)S(1)}, u32[]{:S(2)}, u32[]{:S(2)}) collective-permute-start(f32[9,8,8,128]{3,2,1,0:T(8,128)S(1)} %get-tuple-element.37), channel_id=1, source_target_pairs={{0,1},{1,0},{2,3},{3,2},{4,5},{5,4},{6,7},{7,6},{8,9},{9,8},{10,11... | collective-permute-start | bytes 884744 | tf_op jit(solution)/shard_map/ppermute | solution.py:404
  3.9 7.0 %collective-permute-start.1 = (f32[26,8,128]{2,1,0:T(8,128)S(1)}, f32[26,8,128]{2,1,0:T(8,128)S(1)}, u32[]{:S(2)}, u32[]{:S(2)}) collective-permute-start(f32[26,8,128]{2,1,0:T(8,128)S(1)} %get-tuple-element.39), channel_id=1, source_target_pairs={{0,1},{1,0},{2,4},{3,5},{4,2},{5,3},{6,8},{7,9},{8,6},{9,7},{10,12... | collective-permute-start | bytes 319496 | tf_op jit(solution)/shard_map/ppermute | solution.py:456
  5.4 0.8 %copy-start = (f32[8,16,128]{2,1,0:T(8,128)S(1)}, f32[8,16,128]{2,1,0:T(8,128)}, u32[]{:S(2)}) copy-start(f32[8,16,128]{2,1,0:T(8,128)} %shear_ref.15) | copy-start | bytes 196612
  5.4 5.7 %collective-permute-start.2 = (f32[26,8,128]{2,1,0:T(8,128)S(1)}, f32[26,8,128]{2,1,0:T(8,128)S(1)}, u32[]{:S(2)}, u32[]{:S(2)}) collective-permute-start(f32[26,8,128]{2,1,0:T(8,128)S(1)} %get-tuple-element.40), channel_id=1, source_target_pairs={{0,2},{1,3},{2,0},{3,1},{4,6},{5,7},{6,4},{7,5},{8,10},{9,11},{10,... | collective-permute-start | bytes 319496 | tf_op jit(solution)/shard_map/ppermute | solution.py:457
  11.5 1.6 %collective-permute-start.3 = (f32[9,8,8,128]{3,2,1,0:T(8,128)S(1)}, f32[9,8,8,128]{3,2,1,0:T(8,128)S(1)}, u32[]{:S(2)}, u32[]{:S(2)}) collective-permute-start(f32[9,8,8,128]{3,2,1,0:T(8,128)S(1)} %get-tuple-element.44), channel_id=1, source_target_pairs={{0,1},{1,0},{2,3},{3,2},{4,5},{5,4},{6,7},{7,6},{8,9},{9,8},{10,11... | collective-permute-start | bytes 884744 | tf_op jit(solution)/shard_map/ppermute | solution.py:404
  13.5 7.0 %collective-permute-start.4 = (f32[26,8,128]{2,1,0:T(8,128)S(1)}, f32[26,8,128]{2,1,0:T(8,128)S(1)}, u32[]{:S(2)}, u32[]{:S(2)}) collective-permute-start(f32[26,8,128]{2,1,0:T(8,128)S(1)} %get-tuple-element.46), channel_id=1, source_target_pairs={{0,1},{1,0},{2,4},{3,5},{4,2},{5,3},{6,8},{7,9},{8,6},{9,7},{10,12... | collective-permute-start | bytes 319496 | tf_op jit(solution)/shard_map/ppermute | solution.py:456
  16.1 6.0 %collective-permute-start.5 = (f32[26,8,128]{2,1,0:T(8,128)S(1)}, f32[26,8,128]{2,1,0:T(8,128)S(1)}, u32[]{:S(2)}, u32[]{:S(2)}) collective-permute-start(f32[26,8,128]{2,1,0:T(8,128)S(1)} %get-tuple-element.47), channel_id=1, source_target_pairs={{0,2},{1,3},{2,0},{3,1},{4,6},{5,7},{6,4},{7,5},{8,10},{9,11},{10,... | collective-permute-start | bytes 319496 | tf_op jit(solution)/shard_map/ppermute | solution.py:457
  22.4 1.6 %collective-permute-start.6 = (f32[9,8,8,128]{3,2,1,0:T(8,128)S(1)}, f32[9,8,8,128]{3,2,1,0:T(8,128)S(1)}, u32[]{:S(2)}, u32[]{:S(2)}) collective-permute-start(f32[9,8,8,128]{3,2,1,0:T(8,128)S(1)} %get-tuple-element.52), channel_id=1, source_target_pairs={{0,1},{1,0},{2,3},{3,2},{4,5},{5,4},{6,7},{7,6},{8,9},{9,8},{10,11... | collective-permute-start | bytes 884744 | tf_op jit(solution)/shard_map/ppermute | solution.py:404
  24.5 7.1 %collective-permute-start.7 = (f32[26,8,128]{2,1,0:T(8,128)S(1)}, f32[26,8,128]{2,1,0:T(8,128)S(1)}, u32[]{:S(2)}, u32[]{:S(2)}) collective-permute-start(f32[26,8,128]{2,1,0:T(8,128)S(1)} %get-tuple-element.54), channel_id=1, source_target_pairs={{0,1},{1,0},{2,4},{3,5},{4,2},{5,3},{6,8},{7,9},{8,6},{9,7},{10,12... | collective-permute-start | bytes 319496 | tf_op jit(solution)/shard_map/ppermute | solution.py:456
  26.7 5.7 %collective-permute-start.8 = (f32[26,8,128]{2,1,0:T(8,128)S(1)}, f32[26,8,128]{2,1,0:T(8,128)S(1)}, u32[]{:S(2)}, u32[]{:S(2)}) collective-permute-start(f32[26,8,128]{2,1,0:T(8,128)S(1)} %get-tuple-element.55), channel_id=1, source_target_pairs={{0,2},{1,3},{2,0},{3,1},{4,6},{5,7},{6,4},{7,5},{8,10},{9,11},{10,... | collective-permute-start | bytes 319496 | tf_op jit(solution)/shard_map/ppermute | solution.py:457
  28.1 16.4 %collective-permute-start.11 = (f32[13,4,16,128]{3,2,1,0:T(8,128)S(1)}, f32[13,4,16,128]{3,2,1,0:T(8,128)S(1)}, u32[]{:S(2)}, u32[]{:S(2)}) collective-permute-start(f32[13,4,16,128]{3,2,1,0:T(8,128)S(1)} %get-tuple-element.65), channel_id=1, source_target_pairs={{2,0},{4,2},{6,4},{8,6},{10,8},{12,10},{14,12},{16,14},{18,16},{20... | collective-permute-start | bytes 1277960 | tf_op jit(solution)/shard_map/ppermute | solution.py:467
  32.7 1.6 %collective-permute-start.9 = (f32[9,8,8,128]{3,2,1,0:T(8,128)S(1)}, f32[9,8,8,128]{3,2,1,0:T(8,128)S(1)}, u32[]{:S(2)}, u32[]{:S(2)}) collective-permute-start(f32[9,8,8,128]{3,2,1,0:T(8,128)S(1)} %get-tuple-element.60), channel_id=1, source_target_pairs={{0,1},{1,0},{2,3},{3,2},{4,5},{5,4},{6,7},{7,6},{8,9},{9,8},{10,11... | collective-permute-start | bytes 884744 | tf_op jit(solution)/shard_map/ppermute | solution.py:404
  33.3 17.6 %copy-start.1 = (f32[21,4,16,128]{3,2,1,0:T(8,128)S(1)}, f32[21,4,16,128]{3,2,1,0:T(8,128)}, u32[]{:S(2)}) copy-start(f32[21,4,16,128]{3,2,1,0:T(8,128)} %inflow_ref.1) | copy-start | bytes 2064388
  34.8 16.2 %collective-permute-start.10 = (f32[89,8,128]{2,1,0:T(8,128)S(1)}, f32[89,8,128]{2,1,0:T(8,128)S(1)}, u32[]{:S(2)}, u32[]{:S(2)}) collective-permute-start(f32[89,8,128]{2,1,0:T(8,128)S(1)} %get-tuple-element.64), channel_id=1, source_target_pairs={{2,0},{4,2},{6,4},{8,6},{10,8},{12,10},{14,12},{16,14},{18,16},{20... | collective-permute-start | bytes 1093640 | tf_op jit(solution)/shard_map/ppermute | solution.py:484

commit v3 on v2

--- a/solution.py
+++ b/solution.py
@@ -157,7 +157,8 @@
     return out
 
 
-def first_kernel(per, v_ref, s_ref, rec_ref, mask_ref, w_ref, near_ref, far_ref):
+def first_kernel(per, v_ref, s_ref, rec_ref, mask_ref, *refs):
+    w_ref, near_ref, far_ref = refs[-3:]
     below = mask_ref[0]
     even = mask_ref[3] > 0.5
     for p in range(PLANES):
@@ -200,8 +201,9 @@
 
 
 def second_kernel(
-    per, w_ref, far_ref, near_ref, s_ref, left_ref, shear_ref, mask_ref, v_ref, out_ref, edge_ref, vel
+    per, w_ref, far_ref, near_ref, s_ref, left_ref, shear_ref, mask_ref, v_ref, out_ref, edge_ref, *refs
 ):
+    send_ref, vel = refs[:-1], refs[-1]
     below, sides = mask_ref[0], (mask_ref[1], mask_ref[2])
     even = mask_ref[3] > 0.5
 
@@ -252,9 +254,11 @@
             value = left_ref[k, p] + change[k]
             out_ref[k, p] = value
             edge_ref[3 + k, p] = edge_tile(value)
-
-
-LAST_W, LAST_S, LAST_T, LAST_TAILS = 0, 36, 84, 18
+            if send_ref and p < ADV:
+                send_ref[0][k, p] = value
+
+
+LAST_W, LAST_T, LAST_TAILS = 0, 36, 18
 
 
 def last_first_kernel(per, v_ref, s_ref, rec_ref, mask_ref, unused_ref, w_ref, msg_ref):
@@ -266,10 +270,6 @@
             if p < 6:
                 for h in range(2):
                     msg_ref[LAST_W + 12 * c + 2 * p + h] = made[c][8 * h : 8 * h + 8]
-        if p < ADV:
-            for k in range(6):
-                for h in range(2):
-                    msg_ref[LAST_S + 8 * k + 2 * p + h] = s_ref[k, p, pl.ds(8 * h, 8)]
     tails = [w_ref[c, p, pl.ds(ROWS, TAIL)] for c in range(3) for p in range(ADV)]
     tails += [rec_ref[3 + ACCEL[c][0], p] for c in range(3) for p in range(2)]
     for tile, packed in enumerate(pack_tails(tails, per, mask_ref)):
@@ -287,9 +287,22 @@
             grown_ref[s, p - ADV] = grown[s]
 
 
+def next_plastic_kernel(first_ref, more_ref, tab_ref, mask_ref, inflow_ref, left_ref, grown_ref):
+    inside = jnp.concatenate([mask_ref[2]] * 2, axis=0) > 0.5
+    for p in range(ADV):
+        left, grown = plastic_parts(
+            [first_ref[k, p] for k in range(6)], lambda s: more_ref[s, p], more_ref[12, p], tab_ref
+        )
+        for k in range(6):
+            left_ref[k, p] = left[k]
+        for s in range(12):
+            grown_ref[s, p] = jnp.where(inside, grown[s], inflow_ref[9 + s, p])
+
+
 def last_second_kernel(
-    per, w_ref, msg_ref, more_ref, s_ref, rec_ref, left_ref, grown_ref, shear_ref, tab_ref, mask_ref, inflow_ref,
-    v_out, s_out, d_out, vel, v_ref, out_ref, d_ref, sems,
+    per, w_ref, msg_ref, first_ref, more_ref, s_ref, rec_ref, left_ref, grown_ref, shear_ref, mask_ref, inflow_ref,
+    next_left_ref, next_grown_ref,
+    v_out, s_out, d_out, vel, v_ref, out_ref, sems,
 ):
     copies = []
 
@@ -298,6 +311,7 @@
         copies[-1].start()
 
     write(grown_ref, d_out.at[:, pl.ds(0, ADV)])
+    write(next_grown_ref, d_out.at[:, pl.ds(ADV, ADV)])
     below = mask_ref[0]
     here = jnp.concatenate([mask_ref[2]] * 2, axis=0)
     inside = here > 0.5
@@ -309,7 +323,7 @@
         return unpack_tail(lambda tile: msg_ref[LAST_T + tile], index, per)
 
     def got_stress(k, p):
-        return got(LAST_S + 8 * k + 2 * p, 2)
+        return first_ref[k, p]
 
     for c in range(3):
         ix = ACCEL[c][0]
@@ -349,11 +363,8 @@
             left = [left_ref[k, q] for k in range(6)]
             shear = shear_ref[p]
         else:
-            r = p - PLANES
-            shear = more_ref[12, r]
-            left, grown = plastic_parts(
-                [got_stress(k, r) for k in range(6)], lambda s: more_ref[s, r], shear, tab_ref
-            )
+            left = [next_left_ref[k, p - PLANES] for k in range(6)]
+            shear = more_ref[12, p - PLANES]
         change = stress_change(
             lambda c, o: vel[c, p - 2 + o, pl.ds(0, ROWS)], [vel[c, p - 2] for c in range(3)], shear
         )
@@ -363,10 +374,6 @@
                 value = jnp.where(inside, value, inflow_ref[3 + k, p - PLANES])
             out_ref[k, q] = value
         write(out_ref.at[:, q], s_out.at[:, q])
-        if p >= PLANES:
-            for s in range(12):
-                d_ref[s, p - PLANES] = jnp.where(inside, grown[s], inflow_ref[9 + s, p - PLANES])
-            write(d_ref.at[:, p - PLANES], d_out.at[:, q])
     for copy in copies:
         copy.wait()
 
@@ -452,9 +459,6 @@
     for step in range(STEPS - 1):
         rec = swap_rows(edge)
         message = (24 + -(-6 // per), 8, LANES)
-        w, near, far = call(functools.partial(first_kernel, per), [wide, message, message], (velocity, stress, rec, masks))
-        far = lax.ppermute(far, ("prop", "trans"), far_swap)
-        near = lax.ppermute(near, ("prop", "trans"), near_swap)
         ahead = step == STEPS - 2
         made = call(
             functools.partial(plastic_kernel, ahead),
@@ -463,11 +467,18 @@
             flops=HEAVY,
         )
         left, density = made[:2]
+        w, near, far = call(
+            functools.partial(first_kernel, per),
+            [wide, message, message],
+            (velocity, stress, rec, masks) + ((left,) if ahead else ()),
+        )
+        far = lax.ppermute(far, ("prop", "trans"), far_swap)
+        near = lax.ppermute(near, ("prop", "trans"), near_swap)
         if ahead:
             more = lax.ppermute(made[2], "prop", [(i + 1, i) for i in range(count - 1)])
-        velocity, stress, edge = call(
+        velocity, stress, edge, *first_message = call(
             functools.partial(second_kernel, per),
-            [(3, *shape), (6, *shape), edge_shape],
+            [(3, *shape), (6, *shape), edge_shape] + ([(6, ADV, ROWS, LANES)] if ahead else []),
             (w, far, near, stress, left, shear, masks),
             scratch=[(3, PLANES + 4, EXT, LANES)],
         )
@@ -481,7 +492,12 @@
         [wide, (LAST_T + -(-LAST_TAILS // per), 8, LANES)],
         (velocity, stress, rec, masks, left)
     )
-    message = lax.ppermute(message, "prop", [(i + 1, i) for i in range(count - 1)])
+    down = [(i + 1, i) for i in range(count - 1)]
+    (first,) = (lax.ppermute(m, "prop", down) for m in first_message)
+    message = lax.ppermute(message, "prop", down)
+    next_left, next_grown = call(
+        next_plastic_kernel, [(6, *half), (12, *half)], (first, more, table, masks, inflow), flops=HEAVY
+    )
     shapes = [(3, *shape), (6, *shape), (12, *shape)]
     return tuple(
         pl.pallas_call(
@@ -490,11 +506,11 @@
             out_specs=[pl.BlockSpec(memory_space=pl.ANY)] * 3,
             scratch_shapes=[
                 pltpu.VMEM((3, PLANES + 4, EXT, LANES), F32),
-                *(pltpu.VMEM(d, F32) for d in (*shapes[:2], (12, *half))),
-                pltpu.SemaphoreType.DMA((2 + PLANES + ADV,)),
+                *(pltpu.VMEM(d, F32) for d in shapes[:2]),
+                pltpu.SemaphoreType.DMA((3 + PLANES,)),
             ],
             compiler_params=pltpu.CompilerParams(vmem_limit_bytes=VMEM_LIMIT),
-        )(w, message, more, stress, rec, left, grown, shear, table, masks, inflow)
+        )(w, message, first, more, stress, rec, left, grown, shear, masks, inflow, next_left, next_grown)
     )
 
 

time: 52.8 us -> 66 us (1.25)
  the two profiles are of different devices: /device:TPU:14 before, /device:TPU:20 now
where the time goes in v3:
time: 66 us; the launch traced here: 65.7 us
  starting transfers between devices  34.6 us (52%)
  waiting for transfers between devices  20.9 us (32%)
  Pallas kernels  8.86 us (13%)
  between operations  0.91 us (1%)
    ppermute x1, starting transfers between devices, local(): first, = (lax.ppermute(m, 'prop', down) for m in first_message)  20.6 us
    pallas_call x12, Pallas kernels, call(): pl.pallas_call(kernel, out_shape=[jax.ShapeDtypeStruct(shape, F32) for sh...  6.5 us
    ppermute x3, waiting for transfers between devices, local(): far = lax.ppermute(far, ('prop', 'trans'), far_swap)  6.32 us
    ppermute x1, waiting for transfers between devices, local(): message = lax.ppermute(message, 'prop', down)  5.41 us
    ppermute x3, starting transfers between devices, local(): far = lax.ppermute(far, ('prop', 'trans'), far_swap)  4.87 us
    ppermute x3, waiting for transfers between devices, local(): near = lax.ppermute(near, ('prop', 'trans'), near_swap)  4.48 us
    ppermute x3, starting transfers between devices, local(): near = lax.ppermute(near, ('prop', 'trans'), near_swap)  4.39 us
    ppermute x4, waiting for transfers between devices, swap_rows(): return lax.ppermute(edge, 'trans', [(0, 1), (1, 0)])  4.37 us
  transfers between devices with their start and end apart: 13, of which 12 were waited for; matrix products, arithmetic and copies ran while one was open for 1% of the time, Pallas kernels for 7%

profile of v3, /device:TPU:20, one launch (start us, length us, event | category | flops | bytes accessed | tf_op | source)
XLA Modules:
  0.0 65.7 jit_solution(9234490887868340544)
XLA Ops:
  0.7 1.2 %shard_map.94 = (f32[9,8,8,128]{3,2,1,0:T(8,128)S(1)}, f32[3,8,16,128]{3,2,1,0:T(8,128)S(1)}, f32[6,8,16,128]{3,2,1,0:T(8,128)S(1)}) custom-call(f32[3,8,16,128]{3,2,1,0:T(8,128)} %v_in.1, f32[6,8,16,128]{3,2,1,0:T(8,128)} %s_in.1), custom_call_target="tpu_custom_call" | custom-call | tf_op jit(solution)/shard_map/pallas_call | solution.py:452
  2.3 1.2 %collective-permute-done.rec_ref = f32[9,8,8,128]{3,2,1,0:T(8,128)S(1)} collective-permute-done((f32[9,8,8,128]{3,2,1,0:T(8,128)S(1)}, f32[9,8,8,128]{3,2,1,0:T(8,128)S(1)}, u32[]{:S(2)}, u32[]{:S(2)}) %collective-permute-start) | collective-permute-done | bytes 294944 | tf_op jit(solution)/shard_map/ppermute | solution.py:411
  3.9 1.5 %collective-permute-start.1 = (f32[26,8,128]{2,1,0:T(8,128)S(1)}, f32[26,8,128]{2,1,0:T(8,128)S(1)}, u32[]{:S(2)}, u32[]{:S(2)}) collective-permute-start(f32[26,8,128]{2,1,0:T(8,128)S(1)} %get-tuple-element.42), channel_id=1, source_target_pairs={{0,1},{1,0},{2,4},{3,5},{4,2},{5,3},{6,8},{7,9},{8,6},{9,7},{10,12... | collective-permute-start | bytes 319496 | tf_op jit(solution)/shard_map/ppermute | solution.py:475
  5.4 1.5 %collective-permute-start.2 = (f32[26,8,128]{2,1,0:T(8,128)S(1)}, f32[26,8,128]{2,1,0:T(8,128)S(1)}, u32[]{:S(2)}, u32[]{:S(2)}) collective-permute-start(f32[26,8,128]{2,1,0:T(8,128)S(1)} %get-tuple-element.43), channel_id=1, source_target_pairs={{0,2},{1,3},{2,0},{3,1},{4,6},{5,7},{6,4},{7,5},{8,10},{9,11},{10,... | collective-permute-start | bytes 319496 | tf_op jit(solution)/shard_map/ppermute | solution.py:476
  7.1 1.0 %shard_map.96 = (f32[6,8,16,128]{3,2,1,0:T(8,128)S(1)}, f32[12,8,16,128]{3,2,1,0:T(8,128)S(1)}) custom-call(f32[6,8,16,128]{3,2,1,0:T(8,128)S(1)} %get-tuple-element.39.s_ref, f32[12,8,16,128]{3,2,1,0:T(8,128)S(1)} %copy-done.2, f32[8,16,128]{2,1,0:T(8,128)S(1)} %copy-done, f32[12,6,8,128]{3,2,1,0:T(8,128)S(1)} %broadcast_in_dim.16.tab_ref), custom_call_target="tpu_custom_call" | custom-call | flops 17179869184 | bytes 1048576 | tf_op jit(solution)/shard_map/pallas_call | solution.py:386
  8.1 2.6 %collective-permute-done.1.far_ref = f32[26,8,128]{2,1,0:T(8,128)S(1)} collective-permute-done((f32[26,8,128]{2,1,0:T(8,128)S(1)}, f32[26,8,128]{2,1,0:T(8,128)S(1)}, u32[]{:S(2)}, u32[]{:S(2)}) %collective-permute-start.1) | collective-permute-done | bytes 106528 | tf_op jit(solution)/shard_map/ppermute | solution.py:475
  10.7 1.4 %collective-permute-done.2.near_ref = f32[26,8,128]{2,1,0:T(8,128)S(1)} collective-permute-done((f32[26,8,128]{2,1,0:T(8,128)S(1)}, f32[26,8,128]{2,1,0:T(8,128)S(1)}, u32[]{:S(2)}, u32[]{:S(2)}) %collective-permute-start.2) | collective-permute-done | bytes 106528 | tf_op jit(solution)/shard_map/ppermute | solution.py:476
  12.5 1.6 %collective-permute-done.3.rec_ref = f32[9,8,8,128]{3,2,1,0:T(8,128)S(1)} collective-permute-done((f32[9,8,8,128]{3,2,1,0:T(8,128)S(1)}, f32[9,8,8,128]{3,2,1,0:T(8,128)S(1)}, u32[]{:S(2)}, u32[]{:S(2)}) %collective-permute-start.3) | collective-permute-done | bytes 294944 | tf_op jit(solution)/shard_map/ppermute | solution.py:411
  14.5 1.9 %collective-permute-start.4 = (f32[26,8,128]{2,1,0:T(8,128)S(1)}, f32[26,8,128]{2,1,0:T(8,128)S(1)}, u32[]{:S(2)}, u32[]{:S(2)}) collective-permute-start(f32[26,8,128]{2,1,0:T(8,128)S(1)} %get-tuple-element.49), channel_id=1, source_target_pairs={{0,1},{1,0},{2,4},{3,5},{4,2},{5,3},{6,8},{7,9},{8,6},{9,7},{10,12... | collective-permute-start | bytes 319496 | tf_op jit(solution)/shard_map/ppermute | solution.py:475
  16.3 1.3 %collective-permute-start.5 = (f32[26,8,128]{2,1,0:T(8,128)S(1)}, f32[26,8,128]{2,1,0:T(8,128)S(1)}, u32[]{:S(2)}, u32[]{:S(2)}) collective-permute-start(f32[26,8,128]{2,1,0:T(8,128)S(1)} %get-tuple-element.50), channel_id=1, source_target_pairs={{0,2},{1,3},{2,0},{3,1},{4,6},{5,7},{6,4},{7,5},{8,10},{9,11},{10,... | collective-permute-start | bytes 319496 | tf_op jit(solution)/shard_map/ppermute | solution.py:476
  17.6 1.0 %shard_map.99 = (f32[6,8,16,128]{3,2,1,0:T(8,128)S(1)}, f32[12,8,16,128]{3,2,1,0:T(8,128)S(1)}) custom-call(f32[6,8,16,128]{3,2,1,0:T(8,128)S(1)} %get-tuple-element.46.s_ref, f32[12,8,16,128]{3,2,1,0:T(8,128)S(1)} %get-tuple-element.51.d_ref, f32[8,16,128]{2,1,0:T(8,128)S(1)} %copy-done, f32[12,6,8,128]{3,2,1,0:T(8,128)S(1)} %broadcast_in_dim.16.tab_ref), custom_call_target="tpu_custom_call" | custom-call | flops 17179869184 | bytes 1048576 | tf_op jit(solution)/shard_map/pallas_call | solution.py:386
  18.6 2.6 %collective-permute-done.4.far_ref = f32[26,8,128]{2,1,0:T(8,128)S(1)} collective-permute-done((f32[26,8,128]{2,1,0:T(8,128)S(1)}, f32[26,8,128]{2,1,0:T(8,128)S(1)}, u32[]{:S(2)}, u32[]{:S(2)}) %collective-permute-start.4) | collective-permute-done | bytes 106528 | tf_op jit(solution)/shard_map/ppermute | solution.py:475
  21.2 1.5 %collective-permute-done.5.near_ref = f32[26,8,128]{2,1,0:T(8,128)S(1)} collective-permute-done((f32[26,8,128]{2,1,0:T(8,128)S(1)}, f32[26,8,128]{2,1,0:T(8,128)S(1)}, u32[]{:S(2)}, u32[]{:S(2)}) %collective-permute-start.5) | collective-permute-done | bytes 106528 | tf_op jit(solution)/shard_map/ppermute | solution.py:476
  23.2 1.0 %shard_map.101 = (f32[6,8,16,128]{3,2,1,0:T(8,128)S(1)}, f32[12,8,16,128]{3,2,1,0:T(8,128)S(1)}, f32[13,4,16,128]{3,2,1,0:T(8,128)S(1)}) custom-call(f32[6,8,16,128]{3,2,1,0:T(8,128)S(1)} %get-tuple-element.54.s_ref, f32[12,8,16,128]{3,2,1,0:T(8,128)S(1)} %get-tuple-element.56.d_ref, f32[8,16,128]{2,1,0:T(8,128)S(1)} %copy-done, ...), custom_call_target="tpu_custom_call" | custom-call | flops 17179869184 | bytes 1048576 | tf_op jit(solution)/shard_map/pallas_call | solution.py:386
  25.1 1.5 %collective-permute-start.7 = (f32[26,8,128]{2,1,0:T(8,128)S(1)}, f32[26,8,128]{2,1,0:T(8,128)S(1)}, u32[]{:S(2)}, u32[]{:S(2)}) collective-permute-start(f32[26,8,128]{2,1,0:T(8,128)S(1)} %get-tuple-element.59), channel_id=1, source_target_pairs={{0,1},{1,0},{2,4},{3,5},{4,2},{5,3},{6,8},{7,9},{8,6},{9,7},{10,12... | collective-permute-start | bytes 319496 | tf_op jit(solution)/shard_map/ppermute | solution.py:475
  26.6 1.6 %collective-permute-start.8 = (f32[26,8,128]{2,1,0:T(8,128)S(1)}, f32[26,8,128]{2,1,0:T(8,128)S(1)}, u32[]{:S(2)}, u32[]{:S(2)}) collective-permute-start(f32[26,8,128]{2,1,0:T(8,128)S(1)} %get-tuple-element.60), channel_id=1, source_target_pairs={{0,2},{1,3},{2,0},{3,1},{4,6},{5,7},{6,4},{7,5},{8,10},{9,11},{10,... | collective-permute-start | bytes 319496 | tf_op jit(solution)/shard_map/ppermute | solution.py:476
  28.2 2.6 %collective-permute-start.12 = (f32[13,4,16,128]{3,2,1,0:T(8,128)S(1)}, f32[13,4,16,128]{3,2,1,0:T(8,128)S(1)}, u32[]{:S(2)}, u32[]{:S(2)}) collective-permute-start(f32[13,4,16,128]{3,2,1,0:T(8,128)S(1)} %get-tuple-element.69), channel_id=1, source_target_pairs={{2,0},{4,2},{6,4},{8,6},{10,8},{12,10},{14,12},{16,14},{18,16},{20... | collective-permute-start | bytes 1277960 | tf_op jit(solution)/shard_map/ppermute | solution.py:478
  30.7 1.1 %collective-permute-done.7.far_ref = f32[26,8,128]{2,1,0:T(8,128)S(1)} collective-permute-done((f32[26,8,128]{2,1,0:T(8,128)S(1)}, f32[26,8,128]{2,1,0:T(8,128)S(1)}, u32[]{:S(2)}, u32[]{:S(2)}) %collective-permute-start.7) | collective-permute-done | bytes 106528 | tf_op jit(solution)/shard_map/ppermute | solution.py:475
  31.9 1.5 %collective-permute-done.8.near_ref = f32[26,8,128]{2,1,0:T(8,128)S(1)} collective-permute-done((f32[26,8,128]{2,1,0:T(8,128)S(1)}, f32[26,8,128]{2,1,0:T(8,128)S(1)}, u32[]{:S(2)}, u32[]{:S(2)}) %collective-permute-start.8) | collective-permute-done | bytes 106528 | tf_op jit(solution)/shard_map/ppermute | solution.py:476
  33.7 20.6 %collective-permute-start.11 = (f32[6,4,16,128]{3,2,1,0:T(8,128)S(1)}, f32[6,4,16,128]{3,2,1,0:T(8,128)S(1)}, u32[]{:S(2)}, u32[]{:S(2)}) collective-permute-start(f32[6,4,16,128]{3,2,1,0:T(8,128)S(1)} %get-tuple-element.68), channel_id=1, source_target_pairs={{2,0},{4,2},{6,4},{8,6},{10,8},{12,10},{14,12},{16,14},{18,16},{20... | collective-permute-start | bytes 589832 | tf_op jit(solution)/shard_map/ppermute | solution.py:496
  54.9 1.0 %collective-permute-done.9.rec_ref = f32[9,8,8,128]{3,2,1,0:T(8,128)S(1)} collective-permute-done((f32[9,8,8,128]{3,2,1,0:T(8,128)S(1)}, f32[9,8,8,128]{3,2,1,0:T(8,128)S(1)}, u32[]{:S(2)}, u32[]{:S(2)}) %collective-permute-start.9) | collective-permute-done | bytes 294944 | tf_op jit(solution)/shard_map/ppermute | solution.py:411
  56.3 1.9 %collective-permute-start.10 = (f32[41,8,128]{2,1,0:T(8,128)S(1)}, f32[41,8,128]{2,1,0:T(8,128)S(1)}, u32[]{:S(2)}, u32[]{:S(2)}) collective-permute-start(f32[41,8,128]{2,1,0:T(8,128)S(1)} %get-tuple-element.67), channel_id=1, source_target_pairs={{2,0},{4,2},{6,4},{8,6},{10,8},{12,10},{14,12},{16,14},{18,16},{20... | collective-permute-start | bytes 503816 | tf_op jit(solution)/shard_map/ppermute | solution.py:497
  59.1 5.4 %collective-permute-done.10.msg_ref = f32[41,8,128]{2,1,0:T(8,128)S(1)} collective-permute-done((f32[41,8,128]{2,1,0:T(8,128)S(1)}, f32[41,8,128]{2,1,0:T(8,128)S(1)}, u32[]{:S(2)}, u32[]{:S(2)}) %collective-permute-start.10) | collective-permute-done | bytes 167968 | tf_op jit(solution)/shard_map/ppermute | solution.py:497
  64.6 1.2 %shard_map.107 = (f32[3,8,16,128]{3,2,1,0:T(8,128)}, f32[6,8,16,128]{3,2,1,0:T(8,128)}, f32[12,8,16,128]{3,2,1,0:T(8,128)}) custom-call(f32[3,8,24,128]{3,2,1,0:T(8,128)S(1)} %get-tuple-element.66.w_ref, f32[41,8,128]{2,1,0:T(8,128)S(1)} %collective-permute-done.10.msg_ref, f32[6,4,16,128]{3,2,1,0:T(8,128)S(1)} %collective-permute-done.11.first_ref, ...), custom_call_target="tpu_custom_call" | custom-call | tf_op jit(solution)/shard_map/pallas_call | solution.py:503
  (40 shorter events, 5.1 us)
Async XLA Ops:
  0.6 1.3 %copy-start.3 = (s32[12,3]{0,1:T(4,128)S(1)}, s32[12,3]{0,1:T(4,128)}, u32[]{:S(2)}) copy-start(s32[12,3]{0,1:T(4,128)} %param.11) | copy-start | bytes 436
  0.6 1.3 %copy-start.4 = (s32[12,3]{0,1:T(4,128)S(1)}, s32[12,3]{0,1:T(4,128)}, u32[]{:S(2)}) copy-start(s32[12,3]{0,1:T(4,128)} %param.12) | copy-start | bytes 436
  1.8 5.2 %copy-start.2 = (f32[12,8,16,128]{3,2,1,0:T(8,128)S(1)}, f32[12,8,16,128]{3,2,1,0:T(8,128)}, u32[]{:S(2)}) copy-start(f32[12,8,16,128]{3,2,1,0:T(8,128)} %d_ref.1) | copy-start | bytes 2359300
  1.9 1.6 %collective-permute-start = (f32[9,8,8,128]{3,2,1,0:T(8,128)S(1)}, f32[9,8,8,128]{3,2,1,0:T(8,128)S(1)}, u32[]{:S(2)}, u32[]{:S(2)}) collective-permute-start(f32[9,8,8,128]{3,2,1,0:T(8,128)S(1)} %get-tuple-element.40), channel_id=1, source_target_pairs={{0,1},{1,0},{2,3},{3,2},{4,5},{5,4},{6,7},{7,6},{8,9},{9,8},{10,11... | collective-permute-start | bytes 884744 | tf_op jit(solution)/shard_map/ppermute | solution.py:411
  3.9 6.8 %collective-permute-start.1 = (f32[26,8,128]{2,1,0:T(8,128)S(1)}, f32[26,8,128]{2,1,0:T(8,128)S(1)}, u32[]{:S(2)}, u32[]{:S(2)}) collective-permute-start(f32[26,8,128]{2,1,0:T(8,128)S(1)} %get-tuple-element.42), channel_id=1, source_target_pairs={{0,1},{1,0},{2,4},{3,5},{4,2},{5,3},{6,8},{7,9},{8,6},{9,7},{10,12... | collective-permute-start | bytes 319496 | tf_op jit(solution)/shard_map/ppermute | solution.py:475
  5.4 1.7 %copy-start = (f32[8,16,128]{2,1,0:T(8,128)S(1)}, f32[8,16,128]{2,1,0:T(8,128)}, u32[]{:S(2)}) copy-start(f32[8,16,128]{2,1,0:T(8,128)} %shear_ref.15) | copy-start | bytes 196612
  5.4 6.7 %collective-permute-start.2 = (f32[26,8,128]{2,1,0:T(8,128)S(1)}, f32[26,8,128]{2,1,0:T(8,128)S(1)}, u32[]{:S(2)}, u32[]{:S(2)}) collective-permute-start(f32[26,8,128]{2,1,0:T(8,128)S(1)} %get-tuple-element.43), channel_id=1, source_target_pairs={{0,2},{1,3},{2,0},{3,1},{4,6},{5,7},{6,4},{7,5},{8,10},{9,11},{10,... | collective-permute-start | bytes 319496 | tf_op jit(solution)/shard_map/ppermute | solution.py:476
  12.4 1.6 %collective-permute-start.3 = (f32[9,8,8,128]{3,2,1,0:T(8,128)S(1)}, f32[9,8,8,128]{3,2,1,0:T(8,128)S(1)}, u32[]{:S(2)}, u32[]{:S(2)}) collective-permute-start(f32[9,8,8,128]{3,2,1,0:T(8,128)S(1)} %get-tuple-element.47), channel_id=1, source_target_pairs={{0,1},{1,0},{2,3},{3,2},{4,5},{5,4},{6,7},{7,6},{8,9},{9,8},{10,11... | collective-permute-start | bytes 884744 | tf_op jit(solution)/shard_map/ppermute | solution.py:411
  14.5 6.8 %collective-permute-start.4 = (f32[26,8,128]{2,1,0:T(8,128)S(1)}, f32[26,8,128]{2,1,0:T(8,128)S(1)}, u32[]{:S(2)}, u32[]{:S(2)}) collective-permute-start(f32[26,8,128]{2,1,0:T(8,128)S(1)} %get-tuple-element.49), channel_id=1, source_target_pairs={{0,1},{1,0},{2,4},{3,5},{4,2},{5,3},{6,8},{7,9},{8,6},{9,7},{10,12... | collective-permute-start | bytes 319496 | tf_op jit(solution)/shard_map/ppermute | solution.py:475
  16.3 6.4 %collective-permute-start.5 = (f32[26,8,128]{2,1,0:T(8,128)S(1)}, f32[26,8,128]{2,1,0:T(8,128)S(1)}, u32[]{:S(2)}, u32[]{:S(2)}) collective-permute-start(f32[26,8,128]{2,1,0:T(8,128)S(1)} %get-tuple-element.50), channel_id=1, source_target_pairs={{0,2},{1,3},{2,0},{3,1},{4,6},{5,7},{6,4},{7,5},{8,10},{9,11},{10,... | collective-permute-start | bytes 319496 | tf_op jit(solution)/shard_map/ppermute | solution.py:476
  23.1 1.6 %collective-permute-start.6 = (f32[9,8,8,128]{3,2,1,0:T(8,128)S(1)}, f32[9,8,8,128]{3,2,1,0:T(8,128)S(1)}, u32[]{:S(2)}, u32[]{:S(2)}) collective-permute-start(f32[9,8,8,128]{3,2,1,0:T(8,128)S(1)} %get-tuple-element.55), channel_id=1, source_target_pairs={{0,1},{1,0},{2,3},{3,2},{4,5},{5,4},{6,7},{7,6},{8,9},{9,8},{10,11... | collective-permute-start | bytes 884744 | tf_op jit(solution)/shard_map/ppermute | solution.py:411
  25.1 6.8 %collective-permute-start.7 = (f32[26,8,128]{2,1,0:T(8,128)S(1)}, f32[26,8,128]{2,1,0:T(8,128)S(1)}, u32[]{:S(2)}, u32[]{:S(2)}) collective-permute-start(f32[26,8,128]{2,1,0:T(8,128)S(1)} %get-tuple-element.59), channel_id=1, source_target_pairs={{0,1},{1,0},{2,4},{3,5},{4,2},{5,3},{6,8},{7,9},{8,6},{9,7},{10,12... | collective-permute-start | bytes 319496 | tf_op jit(solution)/shard_map/ppermute | solution.py:475
  26.6 6.8 %collective-permute-start.8 = (f32[26,8,128]{2,1,0:T(8,128)S(1)}, f32[26,8,128]{2,1,0:T(8,128)S(1)}, u32[]{:S(2)}, u32[]{:S(2)}) collective-permute-start(f32[26,8,128]{2,1,0:T(8,128)S(1)} %get-tuple-element.60), channel_id=1, source_target_pairs={{0,2},{1,3},{2,0},{3,1},{4,6},{5,7},{6,4},{7,5},{8,10},{9,11},{10,... | collective-permute-start | bytes 319496 | tf_op jit(solution)/shard_map/ppermute | solution.py:476
  28.2 30.1 %collective-permute-start.12 = (f32[13,4,16,128]{3,2,1,0:T(8,128)S(1)}, f32[13,4,16,128]{3,2,1,0:T(8,128)S(1)}, u32[]{:S(2)}, u32[]{:S(2)}) collective-permute-start(f32[13,4,16,128]{3,2,1,0:T(8,128)S(1)} %get-tuple-element.69), channel_id=1, source_target_pairs={{2,0},{4,2},{6,4},{8,6},{10,8},{12,10},{14,12},{16,14},{18,16},{20... | collective-permute-start | bytes 1277960 | tf_op jit(solution)/shard_map/ppermute | solution.py:478
  33.7 24.9 %collective-permute-start.11 = (f32[6,4,16,128]{3,2,1,0:T(8,128)S(1)}, f32[6,4,16,128]{3,2,1,0:T(8,128)S(1)}, u32[]{:S(2)}, u32[]{:S(2)}) collective-permute-start(f32[6,4,16,128]{3,2,1,0:T(8,128)S(1)} %get-tuple-element.68), channel_id=1, source_target_pairs={{2,0},{4,2},{6,4},{8,6},{10,8},{12,10},{14,12},{16,14},{18,16},{20... | collective-permute-start | bytes 589832 | tf_op jit(solution)/shard_map/ppermute | solution.py:496
  54.3 1.6 %collective-permute-start.9 = (f32[9,8,8,128]{3,2,1,0:T(8,128)S(1)}, f32[9,8,8,128]{3,2,1,0:T(8,128)S(1)}, u32[]{:S(2)}, u32[]{:S(2)}) collective-permute-start(f32[9,8,8,128]{3,2,1,0:T(8,128)S(1)} %get-tuple-element.63), channel_id=1, source_target_pairs={{0,1},{1,0},{2,3},{3,2},{4,5},{5,4},{6,7},{7,6},{8,9},{9,8},{10,11... | collective-permute-start | bytes 884744 | tf_op jit(solution)/shard_map/ppermute | solution.py:411
  54.9 3.7 %copy-start.1 = (f32[21,4,16,128]{3,2,1,0:T(8,128)S(1)}, f32[21,4,16,128]{3,2,1,0:T(8,128)}, u32[]{:S(2)}) copy-start(f32[21,4,16,128]{3,2,1,0:T(8,128)} %inflow_ref.3) | copy-start | bytes 2064388
  56.3 8.2 %collective-permute-start.10 = (f32[41,8,128]{2,1,0:T(8,128)S(1)}, f32[41,8,128]{2,1,0:T(8,128)S(1)}, u32[]{:S(2)}, u32[]{:S(2)}) collective-permute-start(f32[41,8,128]{2,1,0:T(8,128)S(1)} %get-tuple-element.67), channel_id=1, source_target_pairs={{2,0},{4,2},{6,4},{8,6},{10,8},{12,10},{14,12},{16,14},{18,16},{20... | collective-permute-start | bytes 503816 | tf_op jit(solution)/shard_map/ppermute | solution.py:497

commit v4 on v3

--- a/solution.py
+++ b/solution.py
@@ -157,8 +157,7 @@
     return out
 
 
-def first_kernel(per, v_ref, s_ref, rec_ref, mask_ref, *refs):
-    w_ref, near_ref, far_ref = refs[-3:]
+def first_kernel(per, v_ref, s_ref, rec_ref, mask_ref, w_ref, near_ref, far_ref):
     below = mask_ref[0]
     even = mask_ref[3] > 0.5
     for p in range(PLANES):
@@ -459,6 +458,11 @@
     for step in range(STEPS - 1):
         rec = swap_rows(edge)
         message = (24 + -(-6 // per), 8, LANES)
+        w, near, far = call(
+            functools.partial(first_kernel, per), [wide, message, message], (velocity, stress, rec, masks)
+        )
+        far = lax.ppermute(far, ("prop", "trans"), far_swap)
+        near = lax.ppermute(near, ("prop", "trans"), near_swap)
         ahead = step == STEPS - 2
         made = call(
             functools.partial(plastic_kernel, ahead),
@@ -467,13 +471,6 @@
             flops=HEAVY,
         )
         left, density = made[:2]
-        w, near, far = call(
-            functools.partial(first_kernel, per),
-            [wide, message, message],
-            (velocity, stress, rec, masks) + ((left,) if ahead else ()),
-        )
-        far = lax.ppermute(far, ("prop", "trans"), far_swap)
-        near = lax.ppermute(near, ("prop", "trans"), near_swap)
         if ahead:
             more = lax.ppermute(made[2], "prop", [(i + 1, i) for i in range(count - 1)])
         velocity, stress, edge, *first_message = call(

time: 66 us -> 52.4 us (0.79)
  the two profiles are of different devices: /device:TPU:20 before, /device:TPU:14 now
where the time goes in v4:
time: 52.4 us; the launch traced here: 52.1 us
  waiting for transfers between devices  22.9 us (44%)
  starting transfers between devices  18.8 us (36%)
  Pallas kernels  8.86 us (17%)
  between operations  0.92 us (2%)
  local copies, waits for them, and re-layouts  0.56 us (1%)
    pallas_call x12, Pallas kernels, call(): pl.pallas_call(kernel, out_shape=[jax.ShapeDtypeStruct(shape, F32) for sh...  6.5 us
    ppermute x3, starting transfers between devices, local(): far = lax.ppermute(far, ('prop', 'trans'), far_swap)  6.33 us
    ppermute x3, waiting for transfers between devices, local(): far = lax.ppermute(far, ('prop', 'trans'), far_swap)  6.27 us
    ppermute x4, waiting for transfers between devices, swap_rows(): return lax.ppermute(edge, 'trans', [(0, 1), (1, 0)])  5.38 us
    ppermute x1, waiting for transfers between devices, local(): first, = (lax.ppermute(m, 'prop', down) for m in first_message)  4.21 us
    ppermute x1, starting transfers between devices, local(): message = lax.ppermute(message, 'prop', down)  3.69 us
    ppermute x1, starting transfers between devices, local(): more = lax.ppermute(made[2], 'prop', [(i + 1, i) for i in range(count - 1)])  3.46 us
    ppermute x1, starting transfers between devices, local(): first, = (lax.ppermute(m, 'prop', down) for m in first_message)  3.36 us
  transfers between devices with their start and end apart: 13, of which 12 were waited for; matrix products, arithmetic and copies ran while one was open for 1% of the time, Pallas kernels for 9%

profile of v4, /device:TPU:14, one launch (start us, length us, event | category | flops | bytes accessed | tf_op | source)
XLA Modules:
  0.0 52.1 jit_solution(4712566528903762323)
XLA Ops:
  0.7 1.2 %shard_map.94 = (f32[9,8,8,128]{3,2,1,0:T(8,128)S(1)}, f32[3,8,16,128]{3,2,1,0:T(8,128)S(1)}, f32[6,8,16,128]{3,2,1,0:T(8,128)S(1)}) custom-call(f32[3,8,16,128]{3,2,1,0:T(8,128)} %v_in.1, f32[6,8,16,128]{3,2,1,0:T(8,128)} %s_in.1), custom_call_target="tpu_custom_call" | custom-call | tf_op jit(solution)/shard_map/pallas_call | solution.py:451
  2.3 1.2 %collective-permute-done.rec_ref = f32[9,8,8,128]{3,2,1,0:T(8,128)S(1)} collective-permute-done((f32[9,8,8,128]{3,2,1,0:T(8,128)S(1)}, f32[9,8,8,128]{3,2,1,0:T(8,128)S(1)}, u32[]{:S(2)}, u32[]{:S(2)}) %collective-permute-start) | collective-permute-done | bytes 294944 | tf_op jit(solution)/shard_map/ppermute | solution.py:410
  3.9 1.6 %collective-permute-start.1 = (f32[26,8,128]{2,1,0:T(8,128)S(1)}, f32[26,8,128]{2,1,0:T(8,128)S(1)}, u32[]{:S(2)}, u32[]{:S(2)}) collective-permute-start(f32[26,8,128]{2,1,0:T(8,128)S(1)} %get-tuple-element.42), channel_id=1, source_target_pairs={{0,1},{1,0},{2,4},{3,5},{4,2},{5,3},{6,8},{7,9},{8,6},{9,7},{10,12... | collective-permute-start | bytes 319496 | tf_op jit(solution)/shard_map/ppermute | solution.py:464
  6.3 1.0 %shard_map.96 = (f32[6,8,16,128]{3,2,1,0:T(8,128)S(1)}, f32[12,8,16,128]{3,2,1,0:T(8,128)S(1)}) custom-call(f32[6,8,16,128]{3,2,1,0:T(8,128)S(1)} %get-tuple-element.39.s_ref, f32[12,8,16,128]{3,2,1,0:T(8,128)S(1)} %copy-done.2, f32[8,16,128]{2,1,0:T(8,128)S(1)} %copy-done, f32[12,6,8,128]{3,2,1,0:T(8,128)S(1)} %broadcast_in_dim.16.tab_ref), custom_call_target="tpu_custom_call" | custom-call | flops 17179869184 | bytes 1048576 | tf_op jit(solution)/shard_map/pallas_call | solution.py:385
  7.3 3.6 %collective-permute-done.1.far_ref = f32[26,8,128]{2,1,0:T(8,128)S(1)} collective-permute-done((f32[26,8,128]{2,1,0:T(8,128)S(1)}, f32[26,8,128]{2,1,0:T(8,128)S(1)}, u32[]{:S(2)}, u32[]{:S(2)}) %collective-permute-start.1) | collective-permute-done | bytes 106528 | tf_op jit(solution)/shard_map/ppermute | solution.py:464
  11.6 1.6 %collective-permute-done.3.rec_ref = f32[9,8,8,128]{3,2,1,0:T(8,128)S(1)} collective-permute-done((f32[9,8,8,128]{3,2,1,0:T(8,128)S(1)}, f32[9,8,8,128]{3,2,1,0:T(8,128)S(1)}, u32[]{:S(2)}, u32[]{:S(2)}) %collective-permute-start.3) | collective-permute-done | bytes 294944 | tf_op jit(solution)/shard_map/ppermute | solution.py:410
  13.6 2.6 %collective-permute-start.4 = (f32[26,8,128]{2,1,0:T(8,128)S(1)}, f32[26,8,128]{2,1,0:T(8,128)S(1)}, u32[]{:S(2)}, u32[]{:S(2)}) collective-permute-start(f32[26,8,128]{2,1,0:T(8,128)S(1)} %get-tuple-element.49), channel_id=1, source_target_pairs={{0,1},{1,0},{2,4},{3,5},{4,2},{5,3},{6,8},{7,9},{8,6},{9,7},{10,12... | collective-permute-start | bytes 319496 | tf_op jit(solution)/shard_map/ppermute | solution.py:464
  16.1 0.7 %collective-permute-start.5 = (f32[26,8,128]{2,1,0:T(8,128)S(1)}, f32[26,8,128]{2,1,0:T(8,128)S(1)}, u32[]{:S(2)}, u32[]{:S(2)}) collective-permute-start(f32[26,8,128]{2,1,0:T(8,128)S(1)} %get-tuple-element.50), channel_id=1, source_target_pairs={{0,2},{1,3},{2,0},{3,1},{4,6},{5,7},{6,4},{7,5},{8,10},{9,11},{10,... | collective-permute-start | bytes 319496 | tf_op jit(solution)/shard_map/ppermute | solution.py:465
  16.9 1.0 %shard_map.99 = (f32[6,8,16,128]{3,2,1,0:T(8,128)S(1)}, f32[12,8,16,128]{3,2,1,0:T(8,128)S(1)}) custom-call(f32[6,8,16,128]{3,2,1,0:T(8,128)S(1)} %get-tuple-element.46.s_ref, f32[12,8,16,128]{3,2,1,0:T(8,128)S(1)} %get-tuple-element.51.d_ref, f32[8,16,128]{2,1,0:T(8,128)S(1)} %copy-done, f32[12,6,8,128]{3,2,1,0:T(8,128)S(1)} %broadcast_in_dim.16.tab_ref), custom_call_target="tpu_custom_call" | custom-call | flops 17179869184 | bytes 1048576 | tf_op jit(solution)/shard_map/pallas_call | solution.py:385
  17.9 2.7 %collective-permute-done.4.far_ref = f32[26,8,128]{2,1,0:T(8,128)S(1)} collective-permute-done((f32[26,8,128]{2,1,0:T(8,128)S(1)}, f32[26,8,128]{2,1,0:T(8,128)S(1)}, u32[]{:S(2)}, u32[]{:S(2)}) %collective-permute-start.4) | collective-permute-done | bytes 106528 | tf_op jit(solution)/shard_map/ppermute | solution.py:464
  20.5 1.6 %collective-permute-done.5.near_ref = f32[26,8,128]{2,1,0:T(8,128)S(1)} collective-permute-done((f32[26,8,128]{2,1,0:T(8,128)S(1)}, f32[26,8,128]{2,1,0:T(8,128)S(1)}, u32[]{:S(2)}, u32[]{:S(2)}) %collective-permute-start.5) | collective-permute-done | bytes 106528 | tf_op jit(solution)/shard_map/ppermute | solution.py:465
  22.5 1.6 %collective-permute-done.6.rec_ref = f32[9,8,8,128]{3,2,1,0:T(8,128)S(1)} collective-permute-done((f32[9,8,8,128]{3,2,1,0:T(8,128)S(1)}, f32[9,8,8,128]{3,2,1,0:T(8,128)S(1)}, u32[]{:S(2)}, u32[]{:S(2)}) %collective-permute-start.6) | collective-permute-done | bytes 294944 | tf_op jit(solution)/shard_map/ppermute | solution.py:410
  24.5 2.2 %collective-permute-start.7 = (f32[26,8,128]{2,1,0:T(8,128)S(1)}, f32[26,8,128]{2,1,0:T(8,128)S(1)}, u32[]{:S(2)}, u32[]{:S(2)}) collective-permute-start(f32[26,8,128]{2,1,0:T(8,128)S(1)} %get-tuple-element.57), channel_id=1, source_target_pairs={{0,1},{1,0},{2,4},{3,5},{4,2},{5,3},{6,8},{7,9},{8,6},{9,7},{10,12... | collective-permute-start | bytes 319496 | tf_op jit(solution)/shard_map/ppermute | solution.py:464
  27.2 1.0 %shard_map.102 = (f32[6,8,16,128]{3,2,1,0:T(8,128)S(1)}, f32[12,8,16,128]{3,2,1,0:T(8,128)S(1)}, f32[13,4,16,128]{3,2,1,0:T(8,128)S(1)}) custom-call(f32[6,8,16,128]{3,2,1,0:T(8,128)S(1)} %get-tuple-element.54.s_ref, f32[12,8,16,128]{3,2,1,0:T(8,128)S(1)} %get-tuple-element.59.d_ref, f32[8,16,128]{2,1,0:T(8,128)S(1)} %copy-done, ...), custom_call_target="tpu_custom_call" | custom-call | flops 17179869184 | bytes 1048576 | tf_op jit(solution)/shard_map/pallas_call | solution.py:385
  28.2 3.5 %collective-permute-start.12 = (f32[13,4,16,128]{3,2,1,0:T(8,128)S(1)}, f32[13,4,16,128]{3,2,1,0:T(8,128)S(1)}, u32[]{:S(2)}, u32[]{:S(2)}) collective-permute-start(f32[13,4,16,128]{3,2,1,0:T(8,128)S(1)} %get-tuple-element.69), channel_id=1, source_target_pairs={{2,0},{4,2},{6,4},{8,6},{10,8},{12,10},{14,12},{16,14},{18,16},{20... | collective-permute-start | bytes 1277960 | tf_op jit(solution)/shard_map/ppermute | solution.py:475
  31.6 0.8 %collective-permute-done.8.near_ref = f32[26,8,128]{2,1,0:T(8,128)S(1)} collective-permute-done((f32[26,8,128]{2,1,0:T(8,128)S(1)}, f32[26,8,128]{2,1,0:T(8,128)S(1)}, u32[]{:S(2)}, u32[]{:S(2)}) %collective-permute-start.8) | collective-permute-done | bytes 106528 | tf_op jit(solution)/shard_map/ppermute | solution.py:465
  32.8 3.4 %collective-permute-start.11 = (f32[6,4,16,128]{3,2,1,0:T(8,128)S(1)}, f32[6,4,16,128]{3,2,1,0:T(8,128)S(1)}, u32[]{:S(2)}, u32[]{:S(2)}) collective-permute-start(f32[6,4,16,128]{3,2,1,0:T(8,128)S(1)} %get-tuple-element.68), channel_id=1, source_target_pairs={{2,0},{4,2},{6,4},{8,6},{10,8},{12,10},{14,12},{16,14},{18,16},{20... | collective-permute-start | bytes 589832 | tf_op jit(solution)/shard_map/ppermute | solution.py:493
  36.7 1.0 %collective-permute-done.9.rec_ref = f32[9,8,8,128]{3,2,1,0:T(8,128)S(1)} collective-permute-done((f32[9,8,8,128]{3,2,1,0:T(8,128)S(1)}, f32[9,8,8,128]{3,2,1,0:T(8,128)S(1)}, u32[]{:S(2)}, u32[]{:S(2)}) %collective-permute-start.9) | collective-permute-done | bytes 294944 | tf_op jit(solution)/shard_map/ppermute | solution.py:410
  38.2 3.7 %collective-permute-start.10 = (f32[41,8,128]{2,1,0:T(8,128)S(1)}, f32[41,8,128]{2,1,0:T(8,128)S(1)}, u32[]{:S(2)}, u32[]{:S(2)}) collective-permute-start(f32[41,8,128]{2,1,0:T(8,128)S(1)} %get-tuple-element.67), channel_id=1, source_target_pairs={{2,0},{4,2},{6,4},{8,6},{10,8},{12,10},{14,12},{16,14},{18,16},{20... | collective-permute-start | bytes 503816 | tf_op jit(solution)/shard_map/ppermute | solution.py:494
  41.9 2.7 %collective-permute-done.12.more_ref = f32[13,4,16,128]{3,2,1,0:T(8,128)S(1)} collective-permute-done((f32[13,4,16,128]{3,2,1,0:T(8,128)S(1)}, f32[13,4,16,128]{3,2,1,0:T(8,128)S(1)}, u32[]{:S(2)}, u32[]{:S(2)}) %collective-permute-start.12) | collective-permute-done | bytes 426016 | tf_op jit(solution)/shard_map/ppermute | solution.py:475
  44.6 4.2 %collective-permute-done.11.first_ref = f32[6,4,16,128]{3,2,1,0:T(8,128)S(1)} collective-permute-done((f32[6,4,16,128]{3,2,1,0:T(8,128)S(1)}, f32[6,4,16,128]{3,2,1,0:T(8,128)S(1)}, u32[]{:S(2)}, u32[]{:S(2)}) %collective-permute-start.11) | collective-permute-done | bytes 196640 | tf_op jit(solution)/shard_map/ppermute | solution.py:493
  48.8 0.5 shard_map.106
  49.3 1.6 %collective-permute-done.10.msg_ref = f32[41,8,128]{2,1,0:T(8,128)S(1)} collective-permute-done((f32[41,8,128]{2,1,0:T(8,128)S(1)}, f32[41,8,128]{2,1,0:T(8,128)S(1)}, u32[]{:S(2)}, u32[]{:S(2)}) %collective-permute-start.10) | collective-permute-done | bytes 167968 | tf_op jit(solution)/shard_map/ppermute | solution.py:494
  51.0 1.2 %shard_map.107 = (f32[3,8,16,128]{3,2,1,0:T(8,128)}, f32[6,8,16,128]{3,2,1,0:T(8,128)}, f32[12,8,16,128]{3,2,1,0:T(8,128)}) custom-call(f32[3,8,24,128]{3,2,1,0:T(8,128)S(1)} %get-tuple-element.66.w_ref, f32[41,8,128]{2,1,0:T(8,128)S(1)} %collective-permute-done.10.msg_ref, f32[6,4,16,128]{3,2,1,0:T(8,128)S(1)} %collective-permute-done.11.first_ref, ...), custom_call_target="tpu_custom_call" | custom-call | tf_op jit(solution)/shard_map/pallas_call | solution.py:500
  (40 shorter events, 5.2 us)
Async XLA Ops:
  0.6 1.3 %copy-start.3 = (s32[12,3]{0,1:T(4,128)S(1)}, s32[12,3]{0,1:T(4,128)}, u32[]{:S(2)}) copy-start(s32[12,3]{0,1:T(4,128)} %param.11) | copy-start | bytes 436
  0.6 1.3 %copy-start.4 = (s32[12,3]{0,1:T(4,128)S(1)}, s32[12,3]{0,1:T(4,128)}, u32[]{:S(2)}) copy-start(s32[12,3]{0,1:T(4,128)} %param.12) | copy-start | bytes 436
  1.8 4.2 %copy-start.2 = (f32[12,8,16,128]{3,2,1,0:T(8,128)S(1)}, f32[12,8,16,128]{3,2,1,0:T(8,128)}, u32[]{:S(2)}) copy-start(f32[12,8,16,128]{3,2,1,0:T(8,128)} %d_ref.1) | copy-start | bytes 2359300
  1.9 1.6 %collective-permute-start = (f32[9,8,8,128]{3,2,1,0:T(8,128)S(1)}, f32[9,8,8,128]{3,2,1,0:T(8,128)S(1)}, u32[]{:S(2)}, u32[]{:S(2)}) collective-permute-start(f32[9,8,8,128]{3,2,1,0:T(8,128)S(1)} %get-tuple-element.40), channel_id=1, source_target_pairs={{0,1},{1,0},{2,3},{3,2},{4,5},{5,4},{6,7},{7,6},{8,9},{9,8},{10,11... | collective-permute-start | bytes 884744 | tf_op jit(solution)/shard_map/ppermute | solution.py:410
  3.9 7.0 %collective-permute-start.1 = (f32[26,8,128]{2,1,0:T(8,128)S(1)}, f32[26,8,128]{2,1,0:T(8,128)S(1)}, u32[]{:S(2)}, u32[]{:S(2)}) collective-permute-start(f32[26,8,128]{2,1,0:T(8,128)S(1)} %get-tuple-element.42), channel_id=1, source_target_pairs={{0,1},{1,0},{2,4},{3,5},{4,2},{5,3},{6,8},{7,9},{8,6},{9,7},{10,12... | collective-permute-start | bytes 319496 | tf_op jit(solution)/shard_map/ppermute | solution.py:464
  5.4 0.8 %copy-start = (f32[8,16,128]{2,1,0:T(8,128)S(1)}, f32[8,16,128]{2,1,0:T(8,128)}, u32[]{:S(2)}) copy-start(f32[8,16,128]{2,1,0:T(8,128)} %shear_ref.15) | copy-start | bytes 196612
  5.4 5.7 %collective-permute-start.2 = (f32[26,8,128]{2,1,0:T(8,128)S(1)}, f32[26,8,128]{2,1,0:T(8,128)S(1)}, u32[]{:S(2)}, u32[]{:S(2)}) collective-permute-start(f32[26,8,128]{2,1,0:T(8,128)S(1)} %get-tuple-element.43), channel_id=1, source_target_pairs={{0,2},{1,3},{2,0},{3,1},{4,6},{5,7},{6,4},{7,5},{8,10},{9,11},{10,... | collective-permute-start | bytes 319496 | tf_op jit(solution)/shard_map/ppermute | solution.py:465
  11.5 1.6 %collective-permute-start.3 = (f32[9,8,8,128]{3,2,1,0:T(8,128)S(1)}, f32[9,8,8,128]{3,2,1,0:T(8,128)S(1)}, u32[]{:S(2)}, u32[]{:S(2)}) collective-permute-start(f32[9,8,8,128]{3,2,1,0:T(8,128)S(1)} %get-tuple-element.47), channel_id=1, source_target_pairs={{0,1},{1,0},{2,3},{3,2},{4,5},{5,4},{6,7},{7,6},{8,9},{9,8},{10,11... | collective-permute-start | bytes 884744 | tf_op jit(solution)/shard_map/ppermute | solution.py:410
  13.6 7.0 %collective-permute-start.4 = (f32[26,8,128]{2,1,0:T(8,128)S(1)}, f32[26,8,128]{2,1,0:T(8,128)S(1)}, u32[]{:S(2)}, u32[]{:S(2)}) collective-permute-start(f32[26,8,128]{2,1,0:T(8,128)S(1)} %get-tuple-element.49), channel_id=1, source_target_pairs={{0,1},{1,0},{2,4},{3,5},{4,2},{5,3},{6,8},{7,9},{8,6},{9,7},{10,12... | collective-permute-start | bytes 319496 | tf_op jit(solution)/shard_map/ppermute | solution.py:464
  16.1 6.0 %collective-permute-start.5 = (f32[26,8,128]{2,1,0:T(8,128)S(1)}, f32[26,8,128]{2,1,0:T(8,128)S(1)}, u32[]{:S(2)}, u32[]{:S(2)}) collective-permute-start(f32[26,8,128]{2,1,0:T(8,128)S(1)} %get-tuple-element.50), channel_id=1, source_target_pairs={{0,2},{1,3},{2,0},{3,1},{4,6},{5,7},{6,4},{7,5},{8,10},{9,11},{10,... | collective-permute-start | bytes 319496 | tf_op jit(solution)/shard_map/ppermute | solution.py:465
  22.4 1.6 %collective-permute-start.6 = (f32[9,8,8,128]{3,2,1,0:T(8,128)S(1)}, f32[9,8,8,128]{3,2,1,0:T(8,128)S(1)}, u32[]{:S(2)}, u32[]{:S(2)}) collective-permute-start(f32[9,8,8,128]{3,2,1,0:T(8,128)S(1)} %get-tuple-element.55), channel_id=1, source_target_pairs={{0,1},{1,0},{2,3},{3,2},{4,5},{5,4},{6,7},{7,6},{8,9},{9,8},{10,11... | collective-permute-start | bytes 884744 | tf_op jit(solution)/shard_map/ppermute | solution.py:410
  24.5 7.2 %collective-permute-start.7 = (f32[26,8,128]{2,1,0:T(8,128)S(1)}, f32[26,8,128]{2,1,0:T(8,128)S(1)}, u32[]{:S(2)}, u32[]{:S(2)}) collective-permute-start(f32[26,8,128]{2,1,0:T(8,128)S(1)} %get-tuple-element.57), channel_id=1, source_target_pairs={{0,1},{1,0},{2,4},{3,5},{4,2},{5,3},{6,8},{7,9},{8,6},{9,7},{10,12... | collective-permute-start | bytes 319496 | tf_op jit(solution)/shard_map/ppermute | solution.py:464
  26.7 5.7 %collective-permute-start.8 = (f32[26,8,128]{2,1,0:T(8,128)S(1)}, f32[26,8,128]{2,1,0:T(8,128)S(1)}, u32[]{:S(2)}, u32[]{:S(2)}) collective-permute-start(f32[26,8,128]{2,1,0:T(8,128)S(1)} %get-tuple-element.58), channel_id=1, source_target_pairs={{0,2},{1,3},{2,0},{3,1},{4,6},{5,7},{6,4},{7,5},{8,10},{9,11},{10,... | collective-permute-start | bytes 319496 | tf_op jit(solution)/shard_map/ppermute | solution.py:465
  28.2 16.4 %collective-permute-start.12 = (f32[13,4,16,128]{3,2,1,0:T(8,128)S(1)}, f32[13,4,16,128]{3,2,1,0:T(8,128)S(1)}, u32[]{:S(2)}, u32[]{:S(2)}) collective-permute-start(f32[13,4,16,128]{3,2,1,0:T(8,128)S(1)} %get-tuple-element.69), channel_id=1, source_target_pairs={{2,0},{4,2},{6,4},{8,6},{10,8},{12,10},{14,12},{16,14},{18,16},{20... | collective-permute-start | bytes 1277960 | tf_op jit(solution)/shard_map/ppermute | solution.py:475
  32.8 16.1 %collective-permute-start.11 = (f32[6,4,16,128]{3,2,1,0:T(8,128)S(1)}, f32[6,4,16,128]{3,2,1,0:T(8,128)S(1)}, u32[]{:S(2)}, u32[]{:S(2)}) collective-permute-start(f32[6,4,16,128]{3,2,1,0:T(8,128)S(1)} %get-tuple-element.68), channel_id=1, source_target_pairs={{2,0},{4,2},{6,4},{8,6},{10,8},{12,10},{14,12},{16,14},{18,16},{20... | collective-permute-start | bytes 589832 | tf_op jit(solution)/shard_map/ppermute | solution.py:493
  36.1 1.6 %collective-permute-start.9 = (f32[9,8,8,128]{3,2,1,0:T(8,128)S(1)}, f32[9,8,8,128]{3,2,1,0:T(8,128)S(1)}, u32[]{:S(2)}, u32[]{:S(2)}) collective-permute-start(f32[9,8,8,128]{3,2,1,0:T(8,128)S(1)} %get-tuple-element.63), channel_id=1, source_target_pairs={{0,1},{1,0},{2,3},{3,2},{4,5},{5,4},{6,7},{7,6},{8,9},{9,8},{10,11... | collective-permute-start | bytes 884744 | tf_op jit(solution)/shard_map/ppermute | solution.py:410
  36.7 12.1 %copy-start.1 = (f32[21,4,16,128]{3,2,1,0:T(8,128)S(1)}, f32[21,4,16,128]{3,2,1,0:T(8,128)}, u32[]{:S(2)}) copy-start(f32[21,4,16,128]{3,2,1,0:T(8,128)} %inflow_ref.3) | copy-start | bytes 2064388
  38.2 12.8 %collective-permute-start.10 = (f32[41,8,128]{2,1,0:T(8,128)S(1)}, f32[41,8,128]{2,1,0:T(8,128)S(1)}, u32[]{:S(2)}, u32[]{:S(2)}) collective-permute-start(f32[41,8,128]{2,1,0:T(8,128)S(1)} %get-tuple-element.67), channel_id=1, source_target_pairs={{2,0},{4,2},{6,4},{8,6},{10,8},{12,10},{14,12},{16,14},{18,16},{20... | collective-permute-start | bytes 503816 | tf_op jit(solution)/shard_map/ppermute | solution.py:494
